TPU v7x, 256 devices: a whole 4x4x8 slice. The times are simulated.
256 devices in a mesh: sp: 32 (over z, y_hi, core), col: 8 (over y_lo, x).
Axes of the slice: x: 4, y: 4 (y_hi: 2, y_lo: 2; y = y_hi * 2 + y_lo), z: 8, core: 2. Of those that a mesh axis runs over, the one named last changes fastest.
Arguments:
- env_desc: bfloat16 [65536, 3280], P('sp', 'col'), may hold values from -6 to 6
- alpha: float32 [65536], P('sp'), may hold values from -0.0234375 to 0.0234375
- atom_desc: bfloat16 [4096, 3280], P('sp', 'col'), may hold values from -0.109375 to 0.109375
- desc_grad: bfloat16 [4096, 16, 3, 3280], P('sp', None, None, 'col'), may hold values from -0.109375 to 0.109375
- species: int32 [4096], P('sp'), may hold values from 0 to 3
- neighbors: int32 [4096, 16], P('sp'), may hold values from 0 to 383, as said below
Outputs:
- energies: float32 [4096], P('sp')
- forces: float32 [3, 4096], P(None, 'sp')
Inputs may be any that keep to these rules, and one draw needn't show every extreme that they name: `neighbors`: entries lie in 0 to 383 and never name the atom itself (entry 128 + k for the atom at place k of its block); in every block the first slot of the block's first atom is 0 and that of its last atom is 383.
All inputs are finite; a program needn't handle non-finite values.
Results may differ from a plain program's by a relative error of at most 0.007.
Values may be sent and summed in bfloat16 or wider, within the bound.
A program may use at most 128 MiB of HBM per device.

v0:
```python
import jax
import jax.numpy as jnp
from jax import lax
from jax.sharding import PartitionSpec as P


def passed_along(value, axis, by):
    count = lax.axis_size(axis)
    return lax.ppermute(value, axis, [(i, (i + by) % count) for i in range(count)])


def shards(env_desc, alpha, atom_desc, desc_grad, species, neighbors):
    weighted = (alpha[:, None] * env_desc.astype(jnp.float32)).astype(jnp.bfloat16)
    partial_value = lax.dot_general(
        lax.all_gather(env_desc, "col", axis=1, tiled=True),
        weighted,
        (((0,), (0,)), ((), ())),
        preferred_element_type=jnp.float32,
    )
    beta_block = lax.psum(partial_value, "sp").astype(jnp.bfloat16)
    count = atom_desc.shape[0]
    projected = jnp.dot(
        lax.all_gather(atom_desc, "col", axis=1, tiled=True),
        beta_block,
        preferred_element_type=jnp.float32,
    ).astype(jnp.bfloat16)
    active = (species == 0).astype(jnp.float32)
    energy_part = jnp.sum(atom_desc.astype(jnp.float32) * projected.astype(jnp.float32), axis=1)
    pair_part = jnp.einsum("anxc,ac->xna", desc_grad, projected, preferred_element_type=jnp.float32)
    slots = jnp.arange(3 * count, dtype=jnp.int32)
    onehot = (neighbors.T[:, :, None] == slots[None, None, :]).astype(jnp.float32)
    onehot = onehot.reshape(-1, 3 * count)
    energy_sum, pair_sum = lax.psum((energy_part, pair_part), "col")
    masked = pair_sum * active[None, None, :]
    spread = jnp.dot(
        masked.reshape(3, -1),
        onehot,
        precision=lax.Precision.HIGHEST,
        preferred_element_type=jnp.float32,
    )
    own = jnp.sum(masked, axis=1)
    buffer = 2.0 * jnp.pad(own, ((0, 0), (count, count))) - 2.0 * spread
    energies = active * energy_sum
    from_next = passed_along(buffer[:, :count], "sp", -1)
    from_prev = passed_along(buffer[:, 2 * count :], "sp", 1)
    forces = buffer[:, count : 2 * count] + from_next + from_prev
    return (energies, forces)


def solution(mesh):
    placed = (
        P("sp", "col"),
        P("sp"),
        P("sp", "col"),
        P("sp", None, None, "col"),
        P("sp"),
        P("sp", None),
    )
    return jax.shard_map(
        shards, mesh=mesh, in_specs=placed, out_specs=(P("sp"), P(None, "sp")), check_vma=False
    )
```

profile of v0, /device:TPU:1, one launch (start us, length us, event | category | flops | bytes accessed | tf_op | source)
XLA Modules:
  0.0 395.8 jit_solution(7767756022844943364)
XLA Ops:
  7.2 0.0 copy-start.4
  7.2 0.0 all-gather.4.cloned.1.call-start
  7.2 0.7 all-gather.4.cloned.1.call-update
  7.9 27.7 %all-gather.1 = bf16[8,410,128]{2,1,0:T(8,128)(2,1)S(1)} all-gather(bf16[1,410,128]{2,1,0:T(8,128)(2,1)} %bitcast.28), channel_id=1, replica_groups=mesh['sp'=32,'col'=8] {'col'}, dimensions={0}, use_global_device_ids=true | all-gather | bytes 944640 | tf_op jit(solution)/shard_map/all_gather | solution.py:23
  35.6 1.1 reshape.12
  36.7 0.0 copy-done.4
  36.8 0.0 copy-start
  36.8 0.0 copy-start.2
  36.8 123.9 %all-gather.4.cloned.1.call-done = bf16[8,410,2048]{2,1,0:T(8,128)(2,1)} async-done(((bf16[1,410,2048]{2,1,0:T(8,128)(2,1)}), bf16[8,410,2048]{2,1,0:T(8,128)(2,1)}) %all-gather.4.cloned.1.call-update) | async-done | bytes 13434896 | tf_op jit(solution)/shard_map/all_gather | solution.py:15
  160.6 14.9 %reshape.10 = bf16[3280,2048]{1,0:T(8,128)(2,1)} reshape(bf16[8,410,2048]{2,1,0:T(8,128)(2,1)} %all-gather.4.cloned.1.call-done) | data formatting | bytes 26869760
  175.5 0.0 copy-done
  175.5 0.0 copy-done.2
  175.5 11.4 %convolution_bitcast_fusion = f32[3280,410]{0,1:T(8,128)} fusion(bf16[3280,2048]{1,0:T(8,128)(2,1)} %reshape.10, bf16[2048,410]{0,1:T(8,128)(2,1)S(1)} %copy-done, f32[2048]{0:T(1024)S(1)} %copy-done.2), kind=kOutput, calls=%fused_computation.1 | convolution fusion | flops 5510819840 | bytes 20501632 | tf_op jit(solution)/shard_map/dot_general | solution.py:14
  186.9 0.0 copy-start.1
  186.9 157.5 %all-reduce.3 = bf16[3280,410]{0,1:T(8,128)(2,1)S(1)} all-reduce(f32[3280,410]{0,1:T(8,128)} %convolution_bitcast_fusion), channel_id=1, replica_groups=mesh['sp'=32,'col'=8] {'sp'}, use_global_device_ids=true, to_apply=%region_0.0 | all-reduce | flops 1344800 | bytes 8068800 | tf_op jit(solution)/shard_map/psum | solution.py:20
  344.4 0.0 copy-done.1
  344.4 2.1 multiply_reduce_fusion.1
  346.5 0.0 copy-start.3
  346.5 3.4 multiply_reduce_fusion
  349.9 24.7 %all-reduce.1 = (f32[128]{0:T(128)S(1)}, f32[3,16,128]{2,0,1:T(4,128)S(1)}) all-reduce(f32[128]{0:T(128)S(1)} %get-tuple-element.6, f32[3,16,128]{2,0,1:T(4,128)S(1)} %bitcast.29), channel_id=1, replica_groups=mesh['sp'=32,'col'=8] {'col'}, use_global_device_ids=true, to_apply=%region_2.0 | all-reduce | flops 6272 | bytes 50176 | tf_op jit(solution)/shard_map/psum | solution.py:33
  374.7 0.0 copy-done.3
  374.7 1.2 fusion.16
  375.9 11.3 %collective-permute-start = (f32[3,128]{1,0:T(4,128)S(1)}, f32[3,128]{1,0:T(4,128)S(1)}, u32[]{:S(2)}, u32[]{:S(2)}) collective-permute-start(f32[3,128]{1,0:T(4,128)S(1)} %get-tuple-element.4), channel_id=1, source_target_pairs={{0,248},{8,0},{16,8},{24,16},{32,24},{40,32},{48,40},{56,48},{64,5... | collective-permute-start | bytes 4616 | tf_op jit(solution)/shard_map/ppermute | solution.py:9
  387.2 0.0 collective-permute-start.1
  387.2 0.5 compare_select_fusion
  387.7 0.4 collective-permute-done
  388.1 0.3 collective-permute-done.1
  388.4 0.6 fusion.19
  (4 shorter events, 0.0 us)
Async XLA Ops:
  7.2 29.6 %copy-start.4 = (s32[128]{0:T(128)S(1)}, s32[128]{0:T(128)}, u32[]{:S(2)}) copy-start(s32[128]{0:T(128)} %param.10) | copy-start | bytes 1540
  7.2 153.5 %all-gather.4.cloned.1.call-start = ((), (), s32[]{:S(2)}) async-start(), calls=%async_computation | async-start | bytes 15335424 | tf_op jit(solution)/shard_map/all_gather | solution.py:15
  36.8 138.7 %copy-start = (bf16[2048,410]{0,1:T(8,128)(2,1)S(1)}, bf16[2048,410]{0,1:T(8,128)(2,1)}, u32[]{:S(2)}) copy-start(bf16[2048,410]{0,1:T(8,128)(2,1)} %param.6) | copy-start | bytes 5038084
  36.8 138.7 %copy-start.2 = (f32[2048]{0:T(1024)S(1)}, f32[2048]{0:T(1024)}, u32[]{:S(2)}) copy-start(f32[2048]{0:T(1024)} %param.7) | copy-start | bytes 24580
  186.9 157.5 %copy-start.1 = (bf16[128,410]{0,1:T(8,128)(2,1)S(1)}, bf16[128,410]{0,1:T(8,128)(2,1)}, u32[]{:S(2)}) copy-start(bf16[128,410]{0,1:T(8,128)(2,1)} %param.8) | copy-start | bytes 314884
  346.5 28.2 %copy-start.3 = (s32[128,16]{0,1:T(8,128)S(1)}, s32[128,16]{0,1:T(8,128)}, u32[]{:S(2)}) copy-start(s32[128,16]{0,1:T(8,128)} %param.11) | copy-start | bytes 24580
  375.9 12.2 %collective-permute-start = (f32[3,128]{1,0:T(4,128)S(1)}, f32[3,128]{1,0:T(4,128)S(1)}, u32[]{:S(2)}, u32[]{:S(2)}) collective-permute-start(f32[3,128]{1,0:T(4,128)S(1)} %get-tuple-element.4), channel_id=1, source_target_pairs={{0,248},{8,0},{16,8},{24,16},{32,24},{40,32},{48,40},{56,48},{64,5... | collective-permute-start | bytes 4616 | tf_op jit(solution)/shard_map/ppermute | solution.py:9
  387.2 1.2 collective-permute-start.1
Sparse Core Ops, SparseCore 0:
  9.8 150.7 all-gather.3
where the time goes:
time: 400 us; the launch traced here: 396 us
  blocking collectives  210 us (52%)
  waiting for transfers between devices  125 us (31%)
  local copies, waits for them, and re-layouts  16 us (4%)
  matrix products  14.7 us (4%)
  between operations  14.1 us (4%)
  starting transfers between devices  11.4 us (3%)
  other arithmetic  4.56 us (1%)
    psum x1, blocking collectives, shards(): beta_block = lax.psum(partial_value, 'sp').astype(jnp.bfloat16)  157 us
    all_gather x1, waiting for transfers between devices, shards(): lax.all_gather(env_desc, 'col', axis=1, tiled=True)  124 us
    all_gather x1, blocking collectives, shards(): lax.all_gather(atom_desc, 'col', axis=1, tiled=True)  27.7 us
    psum x1, blocking collectives, shards(): energy_sum, pair_sum = lax.psum((energy_part, pair_part), 'col')  24.7 us
    unnamed x12, local copies, waits for them, and re-layouts  16 us
    dot_general x1, matrix products, shards(): lax.dot_general(lax.all_gather(env_desc, 'col', axis=1, tiled=True), weig...  11.4 us
    ppermute x2, starting transfers between devices, passed_along(): lax.ppermute(value, axis, [(i, (i + by) % count) for i in range(count)])  11.3 us
  transfers between devices with their start and end apart: 3, of which 3 were waited for; matrix products, arithmetic and copies ran while one was open for 0% of the time, Pallas kernels for 0%

commit v1 on v0

v1 whole, which is shorter than its diff:
```python
import functools

import jax
import jax.numpy as jnp
from jax import lax
from jax.experimental import pallas as pl
from jax.experimental.pallas import tpu as pltpu
from jax.sharding import PartitionSpec as P

MESH = pl.DeviceIdType.MESH
BF = jnp.bfloat16
F32 = jnp.float32
BLK = 416
SUP = 896
PAN = 7
KH = 1024
WROWS = 2944
CH = 368
NSEM = 128


def kernel(
    env_ref, alpha_ref, at_ref, spec_ref, nb_ref, grad_ref,
    energy_ref, force_ref,
    epad, r0, r1, r2, r3, uw, mine, osend, orecv, rsp, rrp, rsm, rrm,
    csum, ysend, yrecv, ball, ats, grads, onehot, pin, pout, proj, pair_parts, pairs, mrow, fsend, frecv,
    gsem, ssem, rsem,
):
    sp, col = lax.axis_index("sp"), lax.axis_index("col")
    core, yh, z = sp % 2, (sp // 2) % 2, sp // 4
    x, yl = col % 4, col // 4

    def dev(dx=0, fy=0, fh=0, dz=0, fc=0):
        a = 1 - yl if fy else yl
        h = 1 - yh if fh else yh
        k = 1 - core if fc else core
        return ((((z + dz + 8) % 8) * 2 + h) * 2 + k, a * 4 + (x + dx + 4) % 4)

    names = {}

    def copy(name, src, dst, where):
        i = names.setdefault(name, len(names))
        return pltpu.make_async_remote_copy(
            src_ref=src, dst_ref=dst, send_sem=ssem.at[i], recv_sem=rsem.at[i],
            device_id=where, device_id_type=MESH,
        )

    sent = []

    def start(name, src, dst, where):
        c = copy(name, src, dst, where)
        c.start()
        sent.append(c)
        return c

    def al(v, m):
        return pl.multiple_of(v, m)

    grad_copy = pltpu.make_async_copy(grad_ref, grads, gsem)
    grad_copy.start()
    epad[400:416, :] = jnp.zeros((16, 2048), BF)
    epad[0:400, :] = env_ref[0:400, :]
    epad[400:410, :] = env_ref[400:410, :]

    peers = [dev(dx=1), dev(dx=-1), dev(dx=2), dev(fy=1), dev(dx=1, fy=1), dev(dx=-1, fy=1), dev(dx=2, fy=1)]
    peers += [dev(fc=1), dev(dz=1), dev(dz=-1), dev(fh=1), dev(fy=1, fh=1)]
    peers += [dev(dx=1, fy=1, fc=1), dev(dx=-1, fy=1, fc=1), dev(dx=2, fy=1, fc=1)]
    after, before = ((sp + 1) % 32, col), ((sp + 31) % 32, col)
    peers += [after, before]
    barrier = pltpu.get_barrier_semaphore()
    for p in peers:
        pl.semaphore_signal(barrier, inc=1, device_id=p, device_id_type=MESH)
    pl.semaphore_wait(barrier, len(peers))

    mine_k = al(yl * KH, KH)
    their_k = (1 - yl) * KH
    own_rows = pl.ds(al(yl * BLK, 16), BLK)
    oth_rows = pl.ds(al((1 - yl) * BLK, 16), BLK)

    ys = {}
    for q in (0, 2, 1, 3):
        ys[q] = start(f"y{q}", epad.at[:, pl.ds(al(their_k + q * 256, 256), 256)],
                      r0.at[own_rows, pl.ds(q * 256, 256)], dev(fy=1))
    xo_p = start("xop", epad.at[:, pl.ds(al(yl * KH, 512), 512)], r2.at[own_rows, :], dev(dx=1))
    xo_m = start("xom", epad.at[:, pl.ds(al(yl * KH + 512, 512), 512)], r1.at[own_rows, :], dev(dx=-1))

    r0[own_rows, :] = epad[:, pl.ds(mine_k, KH)]
    for r in (r0, r1, r2, r3):
        r[832:896, :] = jnp.zeros((64, r.shape[1]), BF)
    weight = alpha_ref[:, pl.ds(mine_k, KH)]
    uw[own_rows, :] = (r0[own_rows, :].astype(F32) * weight).astype(BF)
    for i in range(4):
        ats[core, i * SUP + 832 : (i + 1) * SUP, :] = jnp.zeros((64, 128), BF)
    slots = lax.broadcasted_iota(jnp.int32, (384, 128), 0)
    for n in range(16):
        onehot[:, n * 128 : (n + 1) * 128] = jnp.where(slots == nb_ref[n : n + 1, :], 1.0, 0.0).astype(BF)
    mrow[...] = jnp.zeros_like(mrow)
    pair_parts[8] = jnp.zeros((56, 128), F32)

    def wave(w, lhs_of, rhs, ks):
        for part in (1, 0):
            rows = pl.ds(al((1 - core if part else core) * BLK, 16), BLK)
            for n0, n in ((0, 256), (256, 256), (512, 256), (768, 128)):
                got = None
                for lhs_lane, rhs_lane, k in ks:
                    d = lax.dot_general(
                        lhs_of[rows, pl.ds(lhs_lane, k)], rhs[n0 : n0 + n, rhs_lane : rhs_lane + k],
                        (((1,), (1,)), ((), ())), preferred_element_type=F32,
                    )
                    got = d if got is None else got + d
                for j in range(n // 128):
                    t = n0 // 128 + j
                    panel = got[:, j * 128 : (j + 1) * 128]
                    if part:
                        osend[w, t * BLK : (t + 1) * BLK, :] = panel.astype(BF)
                    else:
                        mine[w, t * BLK : (t + 1) * BLK, :] = panel
            if part:
                start(f"core{w}", osend.at[w], orecv.at[w], dev(fc=1))

    def chunk(d):
        return pl.ds(al(((d + 8) % 8) * CH, 16), CH)

    def local(w, d):
        return mine[w, chunk(d), :] + orecv[w, chunk(d), :].astype(F32)

    def rs_send(w, s):
        if s < 4:
            v = local(w, z + 4 - s)
            if s:
                live[f"rp{w}{s-1}"].wait_recv()
                v = v + rrp[w, s - 1].astype(F32)
            rsp[w, s] = v.astype(BF)
            live[f"rp{w}{s}"] = start(f"rp{w}{s}", rsp.at[w, s], rrp.at[w, s], dev(dz=1))
        if s < 3:
            v = local(w, z - 3 + s)
            if s:
                live[f"rm{w}{s-1}"].wait_recv()
                v = v + rrm[w, s - 1].astype(F32)
            rsm[w, s] = v.astype(BF)
            live[f"rm{w}{s}"] = start(f"rm{w}{s}", rsm.at[w, s], rrm.at[w, s], dev(dz=-1))

    live = {}

    def core_done(w):
        copy(f"core{w}", osend.at[w], orecv.at[w], dev(fc=1)).wait_recv()

    def rs_end(w):
        live[f"rp{w}3"].wait_recv()
        live[f"rm{w}2"].wait_recv()
        v = local(w, z) + rrp[w, 3].astype(F32) + rrm[w, 2].astype(F32)
        csum[w] = v
        ysend[w] = v.astype(BF)
        a = copy(f"ya{w}", ysend.at[w], yrecv.at[w, 0], dev(fh=1))
        b = copy(f"yb{w}", ysend.at[w], yrecv.at[w, 1], dev(fy=1))
        c = copy(f"yc{w}", ysend.at[w], yrecv.at[w, 2], dev(fy=1, fh=1))

        @pl.when(core == yl)
        def _():
            a.start()

        @pl.when(core != yl)
        def _():
            b.start()
            c.start()

        ycopies.append((a, b, c))

    ycopies = []
    gathers = []

    def ag_start(w):
        a, b, c = ycopies[w]

        @pl.when(core == yl)
        def _():
            a.wait_recv()
            b.wait_recv()
            c.wait_recv()
            v = csum[w] + yrecv[w, 0].astype(F32) + yrecv[w, 1].astype(F32) + yrecv[w, 2].astype(F32)
            ball[w, chunk(z), :] = v.astype(BF)

        ag_step(w, 0)

    def ag_copy(w, s, sign):
        ref = ball.at[w, chunk(z - s if sign > 0 else z + s)]
        return copy(f"g{sign}{w}{s}", ref, ref, dev(dz=sign))

    def ag_recv(w, s, sign):
        ref = ball.at[w, chunk(z - 1 - s if sign > 0 else z + 1 + s)]
        return copy(f"g{sign}{w}{s}", ref, ref, dev(dz=sign))

    def ag_step(w, s):
        @pl.when(core == yl)
        def _():
            if s < 4:
                if s:
                    ag_recv(w, s - 1, 1).wait_recv()
                ag_copy(w, s, 1).start()
            if s < 3:
                if s:
                    ag_recv(w, s - 1, -1).wait_recv()
                ag_copy(w, s, -1).start()

    def ag_end(w):
        @pl.when(core == yl)
        def _():
            ag_recv(w, 3, 1).wait_recv()
            ag_recv(w, 2, -1).wait_recv()

    xp = {}
    for i, q in enumerate((0, 2, 1, 3)):
        ys[q].wait_recv()
        src = r0.at[oth_rows, pl.ds(q * 256, 256)]
        lanes = pl.ds((q % 2) * 256, 256)
        if q < 2:
            xp[q] = start(f"x{q}", src, r2.at[oth_rows, lanes], dev(dx=1))
        else:
            xp[q] = start(f"x{q}", src, r1.at[oth_rows, lanes], dev(dx=-1))
        if i == 1:
            op = al(jnp.where((x + 3) % 4 < 2, 0, 256), 256)
            om = al(jnp.where((x + 1) % 4 < 2, 0, 256), 256)
            xo_p.wait_recv()
            fo_p = start("fop", r2.at[own_rows, pl.ds(op, 256)], r3.at[own_rows, pl.ds(0, 256)], dev(dx=1))
            xo_m.wait_recv()
            fo_m = start("fom", r1.at[own_rows, pl.ds(om, 256)], r3.at[own_rows, pl.ds(256, 256)], dev(dx=-1))
    uw[oth_rows, :] = (r0[oth_rows, :].astype(F32) * weight).astype(BF)
    wave(0, uw, r0, ((0, 0, KH),))
    for q in (0, 1):
        xp[q].wait_recv()
    fp_p = start("fpp", r2.at[oth_rows, pl.ds(op, 256)], r3.at[oth_rows, pl.ds(0, 256)], dev(dx=1))
    for q in (2, 3):
        xp[q].wait_recv()
    fp_m = start("fpm", r1.at[oth_rows, pl.ds(om, 256)], r3.at[oth_rows, pl.ds(256, 256)], dev(dx=-1))
    core_done(0)
    rs_send(0, 0)
    wave(1, uw, r1, ((512, 0, 512),))
    rs_send(0, 1)
    core_done(1)
    rs_send(1, 0)
    wave(2, uw, r2, ((0, 0, 512),))
    rs_send(0, 2)
    core_done(2)
    rs_send(1, 1)
    rs_send(2, 0)
    for c in (fo_p, fo_m, fp_p, fp_m):
        c.wait_recv()
    o3 = jnp.where((x + 2) % 4 < 2, 0, 256)
    wave(3, uw, r3, ((al(o3, 256), 0, 256), (al(o3 + 512, 256), 256, 256)))

    ats[core, pl.ds(al(yl * BLK + 400, 16), 16), :] = jnp.zeros((16, 128), BF)
    ats[core, pl.ds(al(yl * BLK, 16), 400), :] = at_ref[0:400, :]
    ats[core, pl.ds(al(yl * BLK + 400, 16), 10), :] = at_ref[400:410, :]
    own_at = ats.at[core, own_rows, :]
    acopies = []
    for dx, i in ((0, 0), (1, 2), (-1, 1), (2, 3)):
        for fy in (0, 1):
            if dx or fy:
                acopies.append(start(f"a{i}{fy}", own_at, ats.at[core, pl.ds(al(i * SUP + yl * BLK, 16), BLK), :], dev(dx=dx, fy=fy)))

    rs_send(0, 3)
    core_done(3)
    rs_send(1, 2)
    rs_send(2, 1)
    rs_send(3, 0)
    rs_end(0)
    rs_send(1, 3)
    rs_send(2, 2)
    rs_send(3, 1)
    ag_start(0)
    rs_end(1)
    rs_send(2, 3)
    rs_send(3, 2)
    ag_step(0, 1)
    ag_start(1)
    rs_end(2)
    rs_send(3, 3)
    ag_step(0, 2)
    ag_step(1, 1)
    ag_start(2)
    for c in acopies:
        c.wait_recv()
    hand = copy("hand", ats.at[core], ats.at[core], dev(fc=1))

    @pl.when(core != yl)
    def _():
        hand.start()

    rs_end(3)
    ag_step(0, 3)
    ag_step(1, 2)
    ag_step(2, 1)
    ag_start(3)
    ag_end(0)
    ag_step(1, 3)
    ag_step(2, 2)
    ag_step(3, 1)
    ag_end(1)
    ag_step(2, 3)
    ag_step(3, 2)
    ag_end(2)
    ag_step(3, 3)
    ag_end(3)

    pcopies = {}
    for i, dx in ((1, 1), (2, -1), (3, 2)):
        for b in (0, 1):
            pcopies[i, b] = (i, b, dx)
    phand = copy("phand", proj.at[1 - core], proj.at[1 - core], dev(fc=1))

    def p_copy(i, same):
        dx = (0, 1, -1, 2)[i]
        rows = pl.ds(al((i - 1) * SUP + (yl if same else 1 - yl) * BLK, 16), BLK)
        where = dev(dx=dx) if same else dev(dx=dx, fy=1, fc=1)
        return copy(f"p{i}{same}", pout.at[rows, :], pin.at[(i - 1) * 2 + same], where)

    @pl.when(core == yl)
    def _():
        ats_in = copy("hand", ats.at[1 - core], ats.at[1 - core], dev(fc=1))
        ats_in.wait_recv()
        own_atoms = jnp.concatenate([ats[0, own_rows, :], ats[1, own_rows, :]], axis=1)
        for i in (3, 1, 2):
            for t in range(PAN):
                got = lax.dot_general(
                    ball[i, t * BLK : (t + 1) * BLK, :], own_atoms, (((0,), (0,)), ((), ())), preferred_element_type=F32
                )
                pout[(i - 1) * SUP + t * 128 : (i - 1) * SUP + (t + 1) * 128, :] = got.astype(BF)
            for same in (1, 0):
                p_copy(i, same).start()
        total = jnp.zeros((BLK, 256), F32)
        for i in range(4):
            for t in range(PAN):
                rows = slice(i * SUP + t * 128, i * SUP + (t + 1) * 128)
                atoms = jnp.concatenate([ats[0, rows, :], ats[1, rows, :]], axis=1)
                total = total + jnp.dot(ball[i, t * BLK : (t + 1) * BLK, :], atoms, preferred_element_type=F32)
        for i in (1, 2, 3):
            for same in (1, 0):
                p_copy(i, same).wait_recv()
                total = total + pin[(i - 1) * 2 + same].astype(F32)
        proj[0] = total[:, :128].astype(BF)
        proj[1] = total[:, 128:].astype(BF)
        phand.start()

    @pl.when(core != yl)
    def _():
        copy("phand", proj.at[core], proj.at[core], dev(fc=1)).wait_recv()

    grad_copy.wait()
    acc = [jnp.zeros((16, 128), F32) for _ in range(3)]
    energy = jnp.zeros((1, 128), F32)

    def body(step, carry):
        a0, a1, a2, e = carry
        rows = pl.ds(al(step * 16, 16), 16)
        pr = proj[core, rows, :].astype(F32)
        at = ats[core, pl.ds(al(yl * BLK + step * 16, 16), 16), :].astype(F32)
        e = e + jnp.sum(pr * at, axis=0, keepdims=True)
        out = []
        for c, a in enumerate((a0, a1, a2)):
            for r in range(16):
                a = a + grads[c, step * 16 + r].astype(F32) * pr[r : r + 1, :]
            out.append(a)
        return (*out, e)

    a0, a1, a2, energy = lax.fori_loop(0, 25, body, (*acc, energy))
    pr = proj[core, 400:416, :].astype(F32)
    at = ats[core, pl.ds(al(yl * BLK + 400, 16), 16), :].astype(F32)
    energy = energy + jnp.sum(pr * at, axis=0, keepdims=True)
    out = []
    for c, a in enumerate((a0, a1, a2)):
        for r in range(10):
            a = a + grads[c, 400 + r].astype(F32) * pr[r : r + 1, :]
        out.append(a)

    for c in range(3):
        pair_parts[8, c * 16 : (c + 1) * 16, :] = out[c]
    pair_parts[8, 48:49, :] = energy
    scopies = []
    for i, (dx, fy) in enumerate(((1, 0), (-1, 0), (2, 0), (0, 1), (1, 1), (-1, 1), (2, 1))):
        scopies.append(start(f"s{i}", pair_parts.at[8], pair_parts.at[col], dev(dx=dx, fy=fy)))
    pair_parts[col] = pair_parts[8]
    for c in scopies:
        c.wait_recv()
    summed = pair_parts[0]
    for i in range(1, 8):
        summed = summed + pair_parts[i]
    active = jnp.where(spec_ref[...] == 0, 1.0, 0.0)
    energy_ref[...] = summed[48:49, :] * active
    for c in range(3):
        pairs[c] = summed[c * 16 : (c + 1) * 16, :] * active
    own = jnp.sum(pairs[...], axis=1)
    for n in range(16):
        mrow[0:3, n * 128 : (n + 1) * 128] = pairs[:, n, :]
    high = mrow[...].astype(BF)
    low = (mrow[...] - high.astype(F32)).astype(BF)
    dims = (((1,), (1,)), ((), ()))
    spread = lax.dot_general(high, onehot[...], dims, preferred_element_type=F32)
    spread = spread + lax.dot_general(low, onehot[...], dims, preferred_element_type=F32)
    fsend[0] = spread[:, 0:128]
    fsend[1] = spread[:, 256:384]
    fb = start("fb", fsend.at[0], frecv.at[0], before)
    fa = start("fa", fsend.at[1], frecv.at[1], after)
    center = 2.0 * own - 2.0 * spread[0:3, 128:256]
    fb.wait_recv()
    fa.wait_recv()
    force_ref[...] = center - 2.0 * frecv[0, 0:3, :] - 2.0 * frecv[1, 0:3, :]

    for c in sent:
        c.wait_send()

    @pl.when(core == yl)
    def _():
        for w in range(4):
            ycopies[w][0].wait_send()
            for s in range(4):
                ag_copy(w, s, 1).wait_send()
            for s in range(3):
                ag_copy(w, s, -1).wait_send()
        for i in (1, 2, 3):
            for same in (1, 0):
                p_copy(i, same).wait_send()
        phand.wait_send()

    @pl.when(core != yl)
    def _():
        for w in range(4):
            ycopies[w][1].wait_send()
            ycopies[w][2].wait_send()
        hand.wait_send()


def shards(env_desc, alpha, atom_desc, desc_grad, species, neighbors):
    vm = pl.BlockSpec(memory_space=pltpu.VMEM)
    V = pltpu.VMEM
    energies, forces = pl.pallas_call(
        kernel,
        out_shape=(jax.ShapeDtypeStruct((1, 128), F32), jax.ShapeDtypeStruct((3, 128), F32)),
        in_specs=[vm, vm, vm, vm, vm, pl.BlockSpec(memory_space=pl.ANY)],
        out_specs=(vm, vm),
        scratch_shapes=[
            V((BLK, 2048), BF),
            V((SUP, KH), BF), V((SUP, 512), BF), V((SUP, 512), BF), V((SUP, 512), BF),
            V((2 * BLK, KH), BF),
            V((4, WROWS, 128), F32), V((4, WROWS, 128), BF), V((4, WROWS, 128), BF),
            V((4, 4, CH, 128), BF), V((4, 4, CH, 128), BF), V((4, 3, CH, 128), BF), V((4, 3, CH, 128), BF),
            V((4, CH, 128), F32), V((4, CH, 128), BF), V((4, 3, CH, 128), BF),
            V((4, WROWS, 128), BF),
            V((2, 4 * SUP, 128), BF),
            V((3, 410, 16, 128), BF),
            V((384, 2048), BF),
            V((6, BLK, 256), BF), V((3 * SUP, 256), BF), V((2, BLK, 128), BF),
            V((9, 56, 128), F32), V((3, 16, 128), F32), V((8, 2048), F32),
            V((2, 8, 128), F32), V((2, 8, 128), F32),
            pltpu.SemaphoreType.DMA, pltpu.SemaphoreType.DMA((NSEM,)), pltpu.SemaphoreType.DMA((NSEM,)),
        ],
        compiler_params=pltpu.CompilerParams(
            collective_id=0, has_side_effects=True, vmem_limit_bytes=58 * 2**20
        ),
    )(
        env_desc.T,
        alpha[None, :],
        atom_desc.T,
        species[None, :],
        neighbors.T,
        jnp.transpose(desc_grad, (2, 3, 1, 0)),
    )
    return energies.reshape(128), forces


def solution(mesh):
    placed = (
        P("sp", "col"),
        P("sp"),
        P("sp", "col"),
        P("sp", None, None, "col"),
        P("sp"),
        P("sp", None),
    )
    return jax.shard_map(
        shards, mesh=mesh, in_specs=placed, out_specs=(P("sp"), P(None, "sp")), check_vma=False
    )
```

time: 400 us -> 129 us (0.32); the launches traced: 396 us -> 129 us
  blocking collectives: 210 us -> 0 us
  Pallas kernels: 0 us -> 126 us
  waiting for transfers between devices: 125 us -> 0 us
  matrix products: 14.7 us -> 0 us
  local copies, waits for them, and re-layouts: 16 us -> 2.39 us
  between operations: 14.1 us -> 0.64 us
  starting transfers between devices: 11.4 us -> 0 us
  other arithmetic: 4.56 us -> 0 us
    psum x2 -> x0, blocking collectives: 182 us -> none  [the longest x1 157 us: shards(): beta_block = lax.psum(partial_value, 'sp').astype(jnp.bfloat16)]
    pallas_call x0 -> x1, Pallas kernels: none -> 126 us  [shards(): pl.pallas_call(kernel, out_shape=(jax.ShapeDtypeStruct((1, 128), F32), ja...]
    all_gather x1 -> x0, waiting for transfers between devices: 124 us -> none  [shards(): lax.all_gather(env_desc, 'col', axis=1, tiled=True)]
    all_gather x1 -> x0, blocking collectives: 27.7 us -> none  [shards(): lax.all_gather(atom_desc, 'col', axis=1, tiled=True)]
    dot_general x3 -> x0, matrix products: 14.7 us -> none  [the longest x1 11.4 us: shards(): lax.dot_general(lax.all_gather(env_desc, 'col', axis=1, tiled=True), weig...]
    unnamed x12 -> x2, local copies, waits for them, and re-layouts: 16 us -> 2.39 us
    ppermute x2 -> x0, starting transfers between devices: 11.3 us -> none  [passed_along(): lax.ppermute(value, axis, [(i, (i + by) % count) for i in range(count)])]
  transfers between devices with their start and end apart: 3 -> 0, of which waited for: 3 -> 0; matrix products, arithmetic and copies ran while one was open for 0% -> 0% of each run, Pallas kernels for 0% -> 0%
where the time goes in v1:
time: 129 us
  Pallas kernels  126 us (98%)
  local copies, waits for them, and re-layouts  2.39 us (2%)
    pallas_call x1, Pallas kernels, shards(): pl.pallas_call(kernel, out_shape=(jax.ShapeDtypeStruct((1, 128), F32), ja...  126 us

profile of v1, /device:TPU:1, one launch (start us, length us, event | category | flops | bytes accessed | tf_op | source)
XLA Modules:
  0.0 129.1 jit_solution(16925335959844232150)
XLA Ops:
  0.6 126.0 %shard_map.77 = (f32[1,128]{1,0:T(1,128)}, f32[3,128]{1,0:T(4,128)}) custom-call(bf16[410,2048]{1,0:T(8,128)(2,1)} %bitcast.8, f32[1,2048]{1,0:T(1,128)} %bitcast.10, bf16[410,128]{1,0:T(8,128)(2,1)} %bitcast.9, s32[1,128]{1,0:T(1,128)} %bitcast.12, s32[16,128]{1,0:T(8,128)} %bitcast.11, bf16[3,410,16,128]{3,2,1,0:T(8,128)(2,1)} %bitcast.7), custom_call_target="tpu_custom_call" | custom-call | tf_op jit(solution)/shard_map/pallas_call | solution.py:435
  126.7 1.1 copy.10
  127.8 1.2 copy.11

commit v2 on v0

v2 whole, which is shorter than its diff:
```python
import functools

import jax
import jax.numpy as jnp
from jax import lax
from jax.experimental import pallas as pl
from jax.experimental.pallas import tpu as pltpu
from jax.sharding import PartitionSpec as P

MESH = pl.DeviceIdType.MESH
BF = jnp.bfloat16
F32 = jnp.float32
BLK = 416
KC = 512
CHS = (160, 160, 208)
OFF = (0, 1280, 2560)
ROWS = 4224
PANELS = ((0, 1, 2), (3, 4, 5), (6, 7, 8, 9))
STK = 1696
NSEM = 96
NT = (((1,), (1,)), ((), ()))
TN = (((0,), (0,)), ((), ()))


def kernel(
    env_ref, alpha_ref, at_ref, spec_ref, nb_ref, grad_ref,
    out_ref,
    env, r1, r2, relay, part, uw, acc, osend, orecv, rsp, rrp, rsm, rrm, csum, ysend, yrecv, ball,
    ats, astack, arow, grads, onehot, prow, pcol, psend, precv, mout, mrecv, proj, pair_parts, pairs, mrow, fsend, frecv,
    lsem, ssem, rsem,
):
    sp, col = lax.axis_index("sp"), lax.axis_index("col")
    core, yh, z = sp % 2, (sp // 2) % 2, sp // 4
    x, yl = col % 4, col // 4

    def dev(dx=0, fy=0, fh=0, dz=0, fc=0):
        a = 1 - yl if fy else yl
        h = 1 - yh if fh else yh
        k = 1 - core if fc else core
        return ((((z + dz + 8) % 8) * 2 + h) * 2 + k, a * 4 + (x + dx + 4) % 4)

    names = {}
    sent = []

    def copy(name, src, dst, where):
        i = names.setdefault(name, len(names))
        return pltpu.make_async_remote_copy(
            src_ref=src, dst_ref=dst, send_sem=ssem.at[i], recv_sem=rsem.at[i],
            device_id=where, device_id_type=MESH,
        )

    def start(name, src, dst, where):
        c = copy(name, src, dst, where)
        c.start()
        sent.append(c)
        return c

    def al(v, m):
        return pl.multiple_of(v, m)

    env_copy = pltpu.make_async_copy(env_ref, env, lsem.at[0])
    env_copy.start()
    peers = [dev(dx=1), dev(dx=-1), dev(dx=2), dev(fy=1), dev(dx=1, fy=1), dev(dx=-1, fy=1), dev(dx=2, fy=1)]
    peers += [dev(fc=1), dev(fh=1), dev(dz=1), dev(dz=-1)]
    after, before = ((sp + 1) % 32, col), ((sp + 31) % 32, col)
    peers += [after, before]
    barrier = pltpu.get_barrier_semaphore()
    for p in peers:
        pl.semaphore_signal(barrier, inc=1, device_id=p, device_id_type=MESH)
    env_copy.wait()
    grad_copy = pltpu.make_async_copy(grad_ref, grads, lsem.at[1])
    grad_copy.start()
    r1[400:416, :] = jnp.zeros((16, 2048), BF)
    r1[0:400, :] = env[0:400, :]
    r1[400:410, :] = env[400:410, :]
    pl.semaphore_wait(barrier, len(peers))

    def order(at_x):
        t = jnp.where(at_x % 4 >= 2, 0, 1024)
        return [al(o, KC) for o in (t, t + KC, 1024 - t, 1024 - t + KC)]

    ks = order(x)
    ks_left = order(x + 3)
    first = jnp.where(x < 2, 0, 1024)
    own = slice(0, BLK)
    ys, ns, os = [], [], []
    for i in range(4):
        ys.append(start(f"y{i}", r1.at[own, pl.ds(ks[i], KC)], part.at[:, pl.ds(ks[i], KC)], dev(fy=1)))
        ns.append(start(f"n{i}", r1.at[own, pl.ds(ks_left[i], KC)], r1.at[BLK : 2 * BLK, pl.ds(ks_left[i], KC)], dev(dx=-1)))
        os.append(start(f"o{i}", r1.at[own, pl.ds(al(first + i * 256, 256), 256)], relay.at[:, pl.ds(i * 256, 256)], dev(dx=1)))

    def n_wait(i):
        copy(f"n{i}", r1.at[own, pl.ds(ks[i], KC)], r1.at[BLK : 2 * BLK, pl.ds(ks[i], KC)], dev(dx=-1)).wait_recv()

    rs = []

    def pass_on(i):
        os[i].wait_recv()
        rs.append(start(f"r{i}", relay.at[:, pl.ds(i * 256, 256)], r2.at[64 : 64 + BLK, pl.ds(i * 256, 256)], dev(dx=1)))

    r1[832:896, :] = jnp.zeros((64, 2048), BF)
    r2[0:64, :] = jnp.zeros((64, 1024), BF)
    r2[480:512, :] = jnp.zeros((32, 1024), BF)
    uw[0] = (r1[own, :].astype(F32) * alpha_ref[...]).astype(BF)
    slots = lax.broadcasted_iota(jnp.int32, (384, 128), 0)
    for n in range(16):
        onehot[:, n * 128 : (n + 1) * 128] = jnp.where(slots == nb_ref[n : n + 1, :], 1.0, 0.0).astype(BF)
    mrow[...] = jnp.zeros_like(mrow)
    pair_parts[8] = jnp.zeros((56, 128), F32)
    ats[core, 1248:1280, :] = jnp.zeros((32, 128), BF)
    ats[core, 400:416, :] = jnp.zeros((16, 128), BF)
    ats[core, 0:400, :] = at_ref[0:400, :]
    ats[core, 400:410, :] = at_ref[400:410, :]

    def spot(t):
        g = 0 if t < 3 else 1 if t < 6 else 2
        return OFF[g] + (t - PANELS[g][0]) * BLK

    def product(b, k, rhs, r0, n, rk):
        return lax.dot_general(
            uw[b, :, pl.ds(k, KC)], rhs[r0 : r0 + n, pl.ds(rk, KC)], NT, preferred_element_type=F32
        )

    def add(b, t, v, fresh):
        at = slice(spot(t), spot(t) + BLK)
        acc[b, at, :] = v if fresh else acc[b, at, :] + v

    def step(i):
        ys[i].wait_recv()
        n_wait(i)
        k = ks[i]
        uw[1, :, pl.ds(k, KC)] = (part[:, pl.ds(k, KC)].astype(F32) * alpha_ref[:, pl.ds(k, KC)]).astype(BF)
        if i == 3:
            return
        for b in (0, 1):
            for r0, n in ((0, 256), (256, 256), (512, 256), (768, 128)):
                v = product(b, k, r1, r0, n, k)
                for j in range(n // 128):
                    add(b, r0 // 128 + j, v[:, j * 128 : (j + 1) * 128], i == 0)

    def opposite():
        rs[0].wait_recv()
        rs[1].wait_recv()
        for b in (0, 1):
            for r0, n in ((0, 128), (128, 256), (384, 128)):
                v = product(b, ks[0], r2, r0, n, 0)
                for j in range(n // 128):
                    t = 6 + r0 // 128 + j
                    add(b, t, v[:, j * 128 : (j + 1) * 128], t > 6)

    def last(g):
        for other in (1, 0):
            b = 1 - core if other else core
            if g < 2:
                parts = [(PANELS[g][0], ((r1, 3, g * 384, 256, 0),)), (PANELS[g][2], ((r1, 3, g * 384 + 256, 128, 0),))]
            else:
                parts = [
                    (6, ((r1, 3, 768, 128, 0), (r2, 1, 0, 128, 1))),
                    (7, ((r2, 1, 128, 256, 1),)),
                    (9, ((r2, 1, 384, 128, 1),)),
                ]
            for t0, terms in parts:
                v = None
                for rhs, i, r0, n, compact in terms:
                    d = product(b, ks[i], rhs, r0, n, KC if compact else ks[i])
                    v = d if v is None else v + d
                for j in range(n // 128):
                    at = slice(spot(t0 + j), spot(t0 + j) + BLK)
                    full = acc[b, at, :] + v[:, j * 128 : (j + 1) * 128]
                    if other:
                        osend[at, :] = full.astype(BF)
                    else:
                        acc[b, at, :] = full
            if other:
                rows = slice(OFF[g], OFF[g] + 8 * CHS[g])
                cores.append(start(f"core{g}", osend.at[rows, :], orecv.at[rows, :], dev(fc=1)))

    cores = []

    def chunk(g, d):
        return pl.ds(al(OFF[g] + ((d + 8) % 8) * CHS[g], 16), CHS[g])

    def slot(g):
        return slice(OFF[g] // 8, OFF[g] // 8 + CHS[g])

    def local(g, d):
        return acc[core, chunk(g, d), :] + orecv[chunk(g, d), :].astype(F32)

    live = {}

    def ring(g, far):
        return (1 if far == 4 else -1) * (1 if g % 2 == 0 else -1)

    def rs_send(g, s):
        if s == 0:
            cores[g].wait_recv()
        for far, sbuf, rbuf in ((4, rsp, rrp), (3, rsm, rrm)):
            if s >= far:
                continue
            way = ring(g, far)
            v = local(g, z + way * (far - s))
            if s:
                live[g, far, s - 1].wait_recv()
                v = v + rbuf[s - 1, slot(g), :].astype(F32)
            sbuf[s, slot(g), :] = v.astype(BF)
            live[g, far, s] = start(f"s{far}{g}{s}", sbuf.at[s, slot(g), :], rbuf.at[s, slot(g), :], dev(dz=way))

    ycopies = {}

    def rs_end(g):
        live[g, 4, 3].wait_recv()
        live[g, 3, 2].wait_recv()
        v = local(g, z) + rrp[3, slot(g), :].astype(F32) + rrm[2, slot(g), :].astype(F32)
        csum[slot(g), :] = v
        ysend[slot(g), :] = v.astype(BF)
        ycopies[g] = start(f"h{g}", ysend.at[slot(g), :], yrecv.at[slot(g), :], dev(fh=1))

    def ag_start(g):
        ycopies[g].wait_recv()
        ball[chunk(g, z), :] = (csum[slot(g), :] + yrecv[slot(g), :].astype(F32)).astype(BF)
        ag_step(g, 0)

    def ag_copy(g, s, far, recv=0):
        ref = ball.at[chunk(g, z - ring(g, far) * (s + recv)), :]
        return copy(f"g{far}{g}{s}", ref, ref, dev(dz=ring(g, far)))

    def ag_step(g, s):
        for far in (4, 3):
            if s < far:
                if s:
                    ag_copy(g, s - 1, far, 1).wait_recv()
                c = ag_copy(g, s, far)
                c.start()
                sent.append(c)

    def ag_end(g):
        for far in (4, 3):
            ag_copy(g, far - 1, far, 1).wait_recv()

    pass_on(0)
    pass_on(1)
    step(0)
    pass_on(2)
    pass_on(3)
    step(1)
    step(2)
    opposite()
    step(3)
    last(0)
    last(1)
    rs_send(0, 0)
    rs[2].wait_recv()
    rs[3].wait_recv()
    last(2)
    rs_send(1, 0)
    rs_send(2, 0)
    own_at = ats.at[core, own, :]
    acopies = [
        start("an", own_at, ats.at[core, BLK : 2 * BLK, :], dev(dx=-1)),
        start("ao", own_at, ats.at[core, 2 * BLK : 3 * BLK, :], dev(dx=2)),
        start("ap", own_at, ats.at[core, 1280:STK, :], dev(fy=1)),
    ]
    rs_send(0, 1)
    rs_send(1, 1)
    rs_send(2, 1)
    rs_send(0, 2)
    rs_send(1, 2)
    rs_send(2, 2)
    for c in acopies:
        c.wait_recv()
    hand = start("hand", ats.at[core], ats.at[core], dev(fc=1))
    rs_send(0, 3)
    rs_send(1, 3)
    rs_end(0)
    rs_send(2, 3)
    rs_end(1)
    rs_end(2)
    copy("hand", ats.at[1 - core], ats.at[1 - core], dev(fc=1)).wait_recv()
    both = jnp.concatenate([ats[0], ats[1]], axis=1)
    astack[...] = both[0:1280, :]

    @pl.when(core == 0)
    def _():
        arow[...] = both[0:BLK, :]

    @pl.when(core == 1)
    def _():
        arow[...] = both[1280:STK, :]
        astack[0:BLK, :] = jnp.zeros((BLK, 256), BF)

    ag_start(0)
    ag_start(1)
    ag_start(2)
    ag_step(0, 1)
    ag_step(1, 1)
    ag_step(2, 1)
    ag_step(0, 2)
    ag_step(1, 2)
    ag_step(2, 2)
    ag_step(0, 3)
    ag_step(1, 3)

    def p_terms(g):
        total = None
        for t in PANELS[g]:
            beta = ball[spot(t) : spot(t) + BLK, :]
            pcol[t * 128 : (t + 1) * 128, :] = lax.dot_general(beta, arow[...], TN, preferred_element_type=F32)
            d = jnp.dot(beta, astack[t * 128 : (t + 1) * 128, :], preferred_element_type=F32)
            total = d if total is None else total + d
        prow[...] = total if g == 0 else prow[...] + total

    ag_end(0)
    p_terms(0)
    ag_step(2, 3)
    ag_end(1)
    p_terms(1)
    ag_end(2)
    p_terms(2)

    @pl.when(core == 0)
    def _():
        pcol[0:BLK, :] = prow[...]
        pcol[1280:STK, :] = jnp.zeros((BLK, 256), F32)

    @pl.when(core == 1)
    def _():
        pcol[1280:STK, :] = prow[...]

    lanes = pl.ds(al(core * 128, 128), 128)
    psend[...] = pcol[:, pl.ds(al(128 - core * 128, 128), 128)].astype(BF)
    share = start("share", psend, precv, dev(fc=1))
    share.wait_recv()
    mcopies = []
    for i, at, where in ((0, BLK, dev(dx=1)), (1, 2 * BLK, dev(dx=2)), (2, 1280, dev(fy=1))):
        mout[i] = (pcol[at : at + BLK, lanes] + precv[at : at + BLK, :].astype(F32)).astype(BF)
        mcopies.append(start(f"m{i}", mout.at[i], mrecv.at[i], where))
    total = pcol[own, lanes] + precv[own, :].astype(F32)
    for i, c in enumerate(mcopies):
        c.wait_recv()
        total = total + mrecv[i].astype(F32)
    proj[...] = total.astype(BF).astype(F32)

    grad_copy.wait()
    acc = [jnp.zeros((16, 128), F32) for _ in range(3)]
    energy = jnp.zeros((1, 128), F32)

    def body(step, carry):
        a0, a1, a2, e = carry
        rows = pl.ds(al(step * 16, 16), 16)
        pr = proj[rows, :]
        at = ats[core, rows, :].astype(F32)
        e = e + jnp.sum(pr * at, axis=0, keepdims=True)
        out = []
        for c, a in enumerate((a0, a1, a2)):
            for r in range(16):
                a = a + grads[c, step * 16 + r].astype(F32) * pr[r : r + 1, :]
            out.append(a)
        return (*out, e)

    a0, a1, a2, energy = lax.fori_loop(0, 25, body, (*acc, energy))
    pr = proj[400:416, :]
    at = ats[core, 400:416, :].astype(F32)
    energy = energy + jnp.sum(pr * at, axis=0, keepdims=True)
    out = []
    for c, a in enumerate((a0, a1, a2)):
        for r in range(10):
            a = a + grads[c, 400 + r].astype(F32) * pr[r : r + 1, :]
        out.append(a)

    for c in range(3):
        pair_parts[8, c * 16 : (c + 1) * 16, :] = out[c]
    pair_parts[8, 48:49, :] = energy
    scopies = []
    for i, (dx, fy) in enumerate(((1, 0), (-1, 0), (2, 0), (0, 1), (1, 1), (-1, 1), (2, 1))):
        scopies.append(start(f"q{i}", pair_parts.at[8], pair_parts.at[col], dev(dx=dx, fy=fy)))
    pair_parts[col] = pair_parts[8]
    for c in scopies:
        c.wait_recv()
    summed = pair_parts[0]
    for i in range(1, 8):
        summed = summed + pair_parts[i]
    active = jnp.where(spec_ref[...] == 0, 1.0, 0.0)
    out_ref[3:4, :] = summed[48:49, :] * active
    for c in range(3):
        pairs[c] = summed[c * 16 : (c + 1) * 16, :] * active
    own = jnp.sum(pairs[...], axis=1)
    for n in range(16):
        mrow[0:3, n * 128 : (n + 1) * 128] = pairs[:, n, :]
    high = mrow[...].astype(BF)
    low = (mrow[...] - high.astype(F32)).astype(BF)
    dims = (((1,), (1,)), ((), ()))
    spread = lax.dot_general(high, onehot[...], dims, preferred_element_type=F32)
    spread = spread + lax.dot_general(low, onehot[...], dims, preferred_element_type=F32)
    fsend[0] = spread[:, 0:128]
    fsend[1] = spread[:, 256:384]
    fb = start("fb", fsend.at[0], frecv.at[0], before)
    fa = start("fa", fsend.at[1], frecv.at[1], after)
    center = 2.0 * own - 2.0 * spread[0:3, 128:256]
    fb.wait_recv()
    fa.wait_recv()
    out_ref[0:3, :] = center - 2.0 * frecv[0, 0:3, :] - 2.0 * frecv[1, 0:3, :]

    assert len(names) <= NSEM
    for c in sent:
        c.wait_send()


def shards(env_desc, alpha, atom_desc, desc_grad, species, neighbors):
    vm = pl.BlockSpec(memory_space=pltpu.VMEM)
    V = pltpu.VMEM
    out = pl.pallas_call(
        kernel,
        out_shape=jax.ShapeDtypeStruct((4, 128), F32),
        in_specs=[pl.BlockSpec(memory_space=pl.ANY), vm, vm, vm, vm, pl.BlockSpec(memory_space=pl.ANY)],
        out_specs=vm,
        scratch_shapes=[
            V((410, 2048), BF), V((896, 2048), BF), V((512, 1024), BF), V((BLK, 1024), BF), V((BLK, 2048), BF),
            V((2, BLK, 2048), BF), V((2, ROWS, 128), F32), V((ROWS, 128), BF), V((ROWS, 128), BF),
            V((4, 528, 128), BF), V((4, 528, 128), BF), V((3, 528, 128), BF), V((3, 528, 128), BF),
            V((528, 128), F32), V((528, 128), BF), V((528, 128), BF), V((ROWS, 128), BF),
            V((2, STK, 128), BF), V((1280, 256), BF), V((BLK, 256), BF),
            V((3, 410, 16, 128), BF), V((384, 2048), BF),
            V((BLK, 256), F32), V((STK, 256), F32), V((STK, 128), BF), V((STK, 128), BF),
            V((3, BLK, 128), BF), V((3, BLK, 128), BF), V((BLK, 128), F32),
            V((9, 56, 128), F32), V((3, 16, 128), F32), V((8, 2048), F32),
            V((2, 8, 128), F32), V((2, 8, 128), F32),
            pltpu.SemaphoreType.DMA((2,)), pltpu.SemaphoreType.DMA((NSEM,)), pltpu.SemaphoreType.DMA((NSEM,)),
        ],
        compiler_params=pltpu.CompilerParams(
            collective_id=0, has_side_effects=True, vmem_limit_bytes=58 * 2**20
        ),
    )(
        env_desc.T,
        alpha[None, :],
        atom_desc.T,
        species[None, :],
        neighbors.T,
        jnp.transpose(desc_grad, (2, 3, 1, 0)),
    )

    def outputs(both_ref, energy_ref, force_ref):
        energy_ref[...] = both_ref[3:4, :]
        force_ref[...] = both_ref[0:3, :]

    energies, forces = pl.pallas_call(
        outputs, out_shape=(jax.ShapeDtypeStruct((1, 128), F32), jax.ShapeDtypeStruct((3, 128), F32))
    )(out)
    return energies.reshape(128), forces


def solution(mesh):
    placed = (
        P("sp", "col"),
        P("sp"),
        P("sp", "col"),
        P("sp", None, None, "col"),
        P("sp"),
        P("sp", None),
    )
    return jax.shard_map(
        shards, mesh=mesh, in_specs=placed, out_specs=(P("sp"), P(None, "sp")), check_vma=False
    )
```

time: 400 us -> 110 us (0.28); the launches traced: 396 us -> 110 us
  blocking collectives: 210 us -> 0 us
  waiting for transfers between devices: 125 us -> 0 us
  Pallas kernels: 0 us -> 109 us
  local copies, waits for them, and re-layouts: 16 us -> 0 us
  matrix products: 14.7 us -> 0 us
  between operations: 14.1 us -> 0.64 us
  starting transfers between devices: 11.4 us -> 0 us
  other arithmetic: 4.56 us -> 0 us
    psum x2 -> x0, blocking collectives: 182 us -> none  [the longest x1 157 us: shards(): beta_block = lax.psum(partial_value, 'sp').astype(jnp.bfloat16)]
    all_gather x1 -> x0, waiting for transfers between devices: 124 us -> none  [shards(): lax.all_gather(env_desc, 'col', axis=1, tiled=True)]
    pallas_call x0 -> x2, Pallas kernels: none -> 109 us  [the longest x1 108 us: shards(): pl.pallas_call(kernel, out_shape=jax.ShapeDtypeStruct((4, 128), F32), in_...]
    all_gather x1 -> x0, blocking collectives: 27.7 us -> none  [shards(): lax.all_gather(atom_desc, 'col', axis=1, tiled=True)]
    unnamed x12 -> x0, local copies, waits for them, and re-layouts: 16 us -> none
    dot_general x3 -> x0, matrix products: 14.7 us -> none  [the longest x1 11.4 us: shards(): lax.dot_general(lax.all_gather(env_desc, 'col', axis=1, tiled=True), weig...]
    ppermute x2 -> x0, starting transfers between devices: 11.3 us -> none  [passed_along(): lax.ppermute(value, axis, [(i, (i + by) % count) for i in range(count)])]
  transfers between devices with their start and end apart: 3 -> 0, of which waited for: 3 -> 0; matrix products, arithmetic and copies ran while one was open for 0% -> 0% of each run, Pallas kernels for 0% -> 0%
where the time goes in v2:
time: 110 us
  Pallas kernels  109 us (99%)
    pallas_call x1, Pallas kernels, shards(): pl.pallas_call(kernel, out_shape=jax.ShapeDtypeStruct((4, 128), F32), in_...  108 us

profile of v2, /device:TPU:1, one launch (start us, length us, event | category | flops | bytes accessed | tf_op | source)
XLA Modules:
  0.0 110.1 jit_solution(6369031481025992389)
XLA Ops:
  0.6 108.2 %shard_map.77.both_ref = f32[4,128]{1,0:T(4,128)} custom-call(bf16[410,2048]{1,0:T(8,128)(2,1)} %bitcast.8, f32[1,2048]{1,0:T(1,128)} %bitcast.10, bf16[410,128]{1,0:T(8,128)(2,1)} %bitcast.9, s32[1,128]{1,0:T(1,128)} %bitcast.12, s32[16,128]{1,0:T(8,128)} %bitcast.11, bf16[3,410,16,128]{3,2,1,0:T(8,128)(2,1)} %bitcast.7), custom_call_target="tpu_custom_call" | custom-call | tf_op jit(solution)/shard_map/pallas_call | solution.py:411
  108.8 1.3 %shard_map.78 = (f32[1,128]{1,0:T(1,128)}, f32[3,128]{1,0:T(4,128)}) custom-call(f32[4,128]{1,0:T(4,128)} %shard_map.77.both_ref), custom_call_target="tpu_custom_call" | custom-call | tf_op jit(solution)/shard_map/pallas_call | solution.py:445

commit v3 on v2

v3 whole, which is shorter than its diff:
```python
import functools

import jax
import jax.numpy as jnp
from jax import lax
from jax.experimental import pallas as pl
from jax.experimental.pallas import tpu as pltpu
from jax.sharding import PartitionSpec as P

MESH = pl.DeviceIdType.MESH
BF = jnp.bfloat16
F32 = jnp.float32
BLK = 416
LO, HI = 256, 160
KC, KD = 512, 1024
ROW1 = BLK + LO
ROWA, ROWF, ROWH, ROWS = 4 * ROW1, 4 * ROW1 + 4 * HI, 4 * ROW1 + 4 * HI + 2 * BLK, 4608
CHS = (176, 160, 128, 112)
OFF = (0, 8 * 176, ROWA, ROWA + 8 * 128)
NLO, OLO, NHI, OHI, LANES = 416, 768, 1024, 1184, 1408
NSEM = 128
NT = (((1,), (1,)), ((), ()))
TN = (((0,), (0,)), ((), ()))


def kernel(
    env_ref, alpha_hbm, at_hbm, spec_hbm, nb_hbm, grad_ref,
    out_ref,
    alpha_ref, at_ref, spec_ref, nb_ref, env, r1, nhi, olo, ohi, relay_lo, relay_hi, part, uw, acc, osend, orecv, rsp, rrp, rsm, rrm, csum, ysend, yrecv, ball,
    ats, astack, arow, grads, onehot, prow, pcol, pown, psend, precv, mout, mrecv, proj, pairs, mrow, fsend, frecv,
    lsem, ssem, rsem, fsem,
):
    sp, col = lax.axis_index("sp"), lax.axis_index("col")
    core, yh, z = sp % 2, (sp // 2) % 2, sp // 4
    x, yl = col % 4, col // 4

    def dev(dx=0, fy=0, fh=0, dz=0, fc=0):
        a = 1 - yl if fy else yl
        h = 1 - yh if fh else yh
        k = 1 - core if fc else core
        return ((((z + dz + 8) % 8) * 2 + h) * 2 + k, a * 4 + (x + dx + 4) % 4)

    names = {}
    sent = []

    def copy(name, src, dst, where):
        i = names.setdefault(name, len(names))
        return pltpu.make_async_remote_copy(
            src_ref=src, dst_ref=dst, send_sem=ssem.at[i], recv_sem=rsem.at[i],
            device_id=where, device_id_type=MESH,
        )

    def start(name, src, dst, where):
        c = copy(name, src, dst, where)
        c.start()
        sent.append(c)
        return c

    def al(v, m):
        return pl.multiple_of(v, m)

    env_copy = pltpu.make_async_copy(env_ref, env, lsem.at[0])
    env_copy.start()
    small = []
    for i, (src, dst) in enumerate(((alpha_hbm, alpha_ref), (at_hbm, at_ref), (nb_hbm, nb_ref), (spec_hbm, spec_ref))):
        small.append(pltpu.make_async_copy(src, dst, lsem.at[2 + i]))
        small[-1].start()
    peers = [dev(dx=1), dev(dx=-1), dev(dx=2), dev(fy=1), dev(dx=1, fy=1), dev(dx=-1, fy=1), dev(dx=2, fy=1)]
    peers += [dev(fc=1), dev(fh=1), dev(dz=1), dev(dz=-1)]
    across = [(col + j) % 8 for j in range(8)]
    before, after = (sp + 31) % 32, (sp + 1) % 32
    peers += [(s, c) for s in (before, after) for c in across]
    barrier = pltpu.get_barrier_semaphore()
    for p in peers:
        pl.semaphore_signal(barrier, inc=1, device_id=p, device_id_type=MESH)
    env_copy.wait()
    grad_copy = pltpu.make_async_copy(grad_ref, grads, lsem.at[1])
    grad_copy.start()
    r1[400:416, :] = jnp.zeros((16, 2048), BF)
    r1[0:400, :] = env[0:400, :]
    r1[400:410, :] = env[400:410, :]
    pl.semaphore_wait(barrier, len(peers))

    def order(at_x):
        t = jnp.where(at_x % 4 >= 2, 0, 1024)
        return [al(o, KC) for o in (t, t + KC, 1024 - t, 1024 - t + KC)]

    ks = order(x)
    ks_left = order(x + 3)
    kh = [al(ks[0], KD), al(ks[2], KD)]
    kh_left = [al(ks_left[0], KD), al(ks_left[2], KD)]
    first = al(jnp.where(x < 2, 0, 1024), KD)
    own = slice(0, BLK)
    low_rows, high_rows = slice(0, LO), slice(LO, BLK)
    ys, yh_parts, os, rs = [], [], [], []
    for i in range(4):
        ys.append(start(f"y{i}", r1.at[low_rows, pl.ds(ks[i], KC)], part.at[low_rows, pl.ds(ks[i], KC)], dev(fy=1)))
        start(f"n{i}", r1.at[low_rows, pl.ds(ks_left[i], KC)], r1.at[NLO : NLO + LO, pl.ds(ks_left[i], KC)], dev(dx=-1))
        if i < 2:
            os.append(start(f"o{i}", r1.at[low_rows, pl.ds(al(first + i * KC, KC), KC)], relay_lo.at[:, pl.ds(i * KC, KC)], dev(dx=1)))
    for i in range(2):
        yh_parts.append(start(f"yh{i}", r1.at[high_rows, pl.ds(kh[i], KD)], part.at[high_rows, pl.ds(kh[i], KD)], dev(fy=1)))
        start(f"nh{i}", r1.at[high_rows, pl.ds(kh_left[i], KD)], nhi.at[0:HI, pl.ds(kh_left[i], KD)], dev(dx=-1))

    def n_wait(i):
        copy(f"n{i}", r1.at[low_rows, pl.ds(ks[i], KC)], r1.at[NLO : NLO + LO, pl.ds(ks[i], KC)], dev(dx=-1)).wait_recv()

    def nh_wait(i):
        copy(f"nh{i}", r1.at[high_rows, pl.ds(kh[i], KD)], nhi.at[0:HI, pl.ds(kh[i], KD)], dev(dx=-1)).wait_recv()

    def pass_on(i):
        os[i].wait_recv()
        if i < 2:
            rs.append(start(f"r{i}", relay_lo.at[:, pl.ds(i * KC, KC)], olo.at[:, pl.ds(i * KC, KC)], dev(dx=1)))
        else:
            lanes = pl.ds((i - 2) * KC, KC)
            rs.append(start(f"r{i}", relay_hi.at[:, lanes], ohi.at[32 : 32 + HI, lanes], dev(dx=1)))

    def o_high(i):
        lanes = pl.ds((i - 2) * KC, KC)
        src = r1.at[high_rows, pl.ds(al(first + (i - 2) * KC, KC), KC)]
        os.append(start(f"o{i}", src, relay_hi.at[:, lanes], dev(dx=1)))

    r1[NLO + LO : OLO, :] = jnp.zeros((OLO - NLO - LO, 2048), BF)
    nhi[HI:256, :] = jnp.zeros((256 - HI, 2048), BF)
    ohi[0:32, :] = jnp.zeros((32, 1024), BF)
    ohi[32 + HI : 256, :] = jnp.zeros((224 - HI, 1024), BF)
    for c in small:
        c.wait()
    uw[own, :] = (r1[own, :].astype(F32) * alpha_ref[...]).astype(BF)
    slots = lax.broadcasted_iota(jnp.int32, (384, 128), 0)
    for n in range(16):
        onehot[:, n * 128 : (n + 1) * 128] = jnp.where(slots == nb_ref[n : n + 1, :], 1.0, 0.0).astype(BF)
    mrow[...] = jnp.zeros_like(mrow)
    prow[...] = jnp.zeros_like(prow)
    pcol[...] = jnp.zeros_like(pcol)
    for c in (0, 1):
        acc[c, ROWH + BLK : ROWS, :] = jnp.zeros((ROWS - ROWH - BLK, 128), F32)
    ats[core, 400:416, :] = jnp.zeros((16, 128), BF)
    ats[core, 0:400, :] = at_ref[0:400, :]
    ats[core, 400:410, :] = at_ref[400:410, :]

    filled = set()

    def add(c, row, v):
        at = slice(row, row + v.shape[0])
        acc[c, at, :] = acc[c, at, :] + v if (c, row) in filled else v
        filled.add((c, row))

    def weigh(rows, k, n):
        at = slice(BLK + rows.start, BLK + rows.stop)
        uw[at, pl.ds(k, n)] = (part[rows, pl.ds(k, n)].astype(F32) * alpha_ref[:, pl.ds(k, n)]).astype(BF)

    def product(rows, rhs, r0, k, rk, n):
        return lax.dot_general(
            uw[rows, pl.ds(k, n)], rhs[r0 : r0 + 256, pl.ds(rk, n)], NT, preferred_element_type=F32
        )

    def panels(v, t, base, stride):
        for j in (0, 1):
            add((t + j) // 4, base + (t + j) % 4 * stride, v[:, j * 128 : (j + 1) * 128])

    front, back, every = slice(0, ROW1), slice(ROW1, 2 * BLK), slice(0, 2 * BLK)

    def low_step(i):
        ys[i].wait_recv()
        n_wait(i)
        weigh(low_rows, ks[i], KC)
        for t in (0, 2, 4):
            panels(product(front, r1, t * 128, ks[i], ks[i], KC), t, 0, ROW1)

    def low_opposite(j):
        rs[j].wait_recv()
        panels(product(front, olo, 0, ks[j], j * KC, KC), 6, 0, ROW1)

    def high_step(i):
        yh_parts[i].wait_recv()
        nh_wait(i)
        weigh(high_rows, kh[i], KD)
        for t in (0, 2, 4):
            panels(product(back, r1, t * 128, kh[i], kh[i], KD), t, ROWA, HI)
        if i == 0:
            panels(product(back, olo, 0, kh[0], 0, KD), 6, ROWA, HI)
        v = product(every, nhi, 0, kh[i], kh[i], KD)
        add(0, ROWF, v[:, 0:128])
        add(0, ROWH, v[0:BLK, 128:256])
        add(1, ROWH, v[BLK : 2 * BLK, 128:256])

    def high_opposite():
        rs[2].wait_recv()
        rs[3].wait_recv()
        v = product(every, ohi, 0, kh[0], 0, KD)
        add(0, ROWH, v[0:BLK, 0:128])
        add(1, ROWH, v[BLK : 2 * BLK, 0:128])
        add(1, ROWF, v[:, 128:256])

    cores = []

    def core_send(rows):
        osend[rows, :] = acc[1 - core, rows, :].astype(BF)
        cores.append(start(f"core{rows.start}", osend.at[rows, :], orecv.at[rows, :], dev(fc=1)))

    def chunk(g, d):
        return pl.ds(al(OFF[g] + ((d + 8) % 8) * CHS[g], 16), CHS[g])

    def slot(g):
        return slice(OFF[g] // 8, OFF[g] // 8 + CHS[g])

    def local(g, d):
        return acc[core, chunk(g, d), :] + orecv[chunk(g, d), :].astype(F32)

    live = {}

    def ring(g, far):
        return (1 if far == 4 else -1) * (1 if g % 2 == 0 else -1)

    def rs_send(g, s):
        if s == 0 and g % 2 == 0:
            cores[g // 2].wait_recv()
        for far, sbuf, rbuf in ((4, rsp, rrp), (3, rsm, rrm)):
            if s >= far:
                continue
            way = ring(g, far)
            v = local(g, z + way * (far - s))
            if s:
                live[g, far, s - 1].wait_recv()
                v = v + rbuf[s - 1, slot(g), :].astype(F32)
            sbuf[s, slot(g), :] = v.astype(BF)
            live[g, far, s] = start(f"s{far}{g}{s}", sbuf.at[s, slot(g), :], rbuf.at[s, slot(g), :], dev(dz=way))

    ycopies = {}

    def rs_end(g):
        live[g, 4, 3].wait_recv()
        live[g, 3, 2].wait_recv()
        v = local(g, z) + rrp[3, slot(g), :].astype(F32) + rrm[2, slot(g), :].astype(F32)
        csum[slot(g), :] = v
        ysend[slot(g), :] = v.astype(BF)
        ycopies[g] = start(f"h{g}", ysend.at[slot(g), :], yrecv.at[slot(g), :], dev(fh=1))

    def ag_start(g):
        ycopies[g].wait_recv()
        ball[chunk(g, z), :] = (csum[slot(g), :] + yrecv[slot(g), :].astype(F32)).astype(BF)
        ag_step(g, 0)

    def ag_copy(g, s, far, recv=0):
        ref = ball.at[chunk(g, z - ring(g, far) * (s + recv)), :]
        return copy(f"g{far}{g}{s}", ref, ref, dev(dz=ring(g, far)))

    def ag_step(g, s):
        for far in (4, 3):
            if s < far:
                if s:
                    ag_copy(g, s - 1, far, 1).wait_recv()
                c = ag_copy(g, s, far)
                c.start()
                sent.append(c)

    def ag_end(g):
        for far in (4, 3):
            ag_copy(g, far - 1, far, 1).wait_recv()

    pass_on(0)
    o_high(2)
    low_step(0)
    pass_on(1)
    o_high(3)
    low_step(1)
    low_step(2)
    low_opposite(0)
    low_step(3)
    low_opposite(1)
    core_send(slice(0, ROWA))
    pass_on(2)
    rs_send(0, 0)
    rs_send(1, 0)
    pass_on(3)
    rs_send(0, 1)
    rs_send(1, 1)
    high_step(0)
    rs_send(0, 2)
    rs_send(1, 2)
    high_step(1)
    high_opposite()
    core_send(slice(ROWA, ROWS))
    own_at = ats.at[core, own, :]
    acopies = [
        start("an", own_at, ats.at[core, BLK : 2 * BLK, :], dev(dx=-1)),
        start("ao", own_at, ats.at[core, 2 * BLK : 3 * BLK, :], dev(dx=2)),
        start("ap", own_at, ats.at[core, 3 * BLK : 4 * BLK, :], dev(fy=1)),
    ]
    rs_send(0, 3)
    rs_send(1, 3)
    rs_send(2, 0)
    rs_send(3, 0)
    rs_end(0)
    rs_end(1)
    rs_send(2, 1)
    rs_send(3, 1)
    ag_start(0)
    ag_start(1)
    rs_send(2, 2)
    rs_send(3, 2)
    ag_step(0, 1)
    ag_step(1, 1)
    for c in acopies:
        c.wait_recv()
    hand = start("hand", ats.at[core], ats.at[core], dev(fc=1))
    rs_send(2, 3)
    rs_send(3, 3)
    ag_step(0, 2)
    ag_step(1, 2)
    rs_end(2)
    rs_end(3)
    ag_step(0, 3)
    ag_step(1, 3)
    copy("hand", ats.at[1 - core], ats.at[1 - core], dev(fc=1)).wait_recv()

    def block(i, rows=own):
        return slice(i * BLK + rows.start, i * BLK + rows.stop)

    both = jnp.concatenate([ats[0], ats[1]], axis=1)
    arow[own, :] = both[block(0), :]
    arow[BLK : 2 * BLK, :] = both[block(3), :]
    astack[own, :] = both[block(0), :]
    astack[NLO : NLO + LO, :] = both[block(1, low_rows), :]
    astack[NLO + LO : OLO, :] = jnp.zeros((OLO - NLO - LO, 256), BF)
    astack[OLO:NHI, :] = both[block(2, low_rows), :]
    astack[NHI:OHI, :] = both[block(1, high_rows), :]
    astack[OHI : OHI + HI, :] = both[block(2, high_rows), :]
    astack[OHI + HI : LANES, :] = jnp.zeros((LANES - OHI - HI, 256), BF)
    ag_start(2)
    ag_start(3)

    def dot(a, b):
        return jnp.dot(a, b, preferred_element_type=F32)

    def turned(a, b):
        return lax.dot_general(a, b, TN, preferred_element_type=F32)

    def p_first():
        ag_end(0)
        ag_end(1)

        @pl.when(core == 0)
        def _():
            total = jnp.zeros((BLK, 256), F32)
            for q in range(4):
                own_part = ball[q * ROW1 : q * ROW1 + BLK, :]
                partner = ball[q * ROW1 + BLK : (q + 1) * ROW1, :]
                at = slice(q * 128, (q + 1) * 128)
                total = total + dot(own_part, astack[at, :])
                terms = turned(partner, arow[BLK:ROW1, :])
                if q == 3:
                    next_only = lax.broadcasted_iota(jnp.int32, (128, 256), 0) >= BLK - 384
                    terms = terms + jnp.where(next_only, turned(own_part, arow[own, :]), 0.0)
                    prow[BLK:ROW1, :] = dot(partner, jnp.where(next_only, astack[at, :].astype(F32), 0.0).astype(BF))
                pcol[at, :] = terms
            prow[own, :] = total

        @pl.when(core == 1)
        def _():
            total = jnp.zeros((ROW1, 256), F32)
            for q in range(4):
                beta = ball[q * ROW1 : (q + 1) * ROW1, :]
                at = slice((4 + q) * 128, (5 + q) * 128)
                total = total + dot(beta, astack[at, :])
                pcol[at, :] = turned(beta, arow[front, :])
            prow[front, :] = total

    def p_second():
        ag_end(2)
        ag_end(3)
        full = ball[ROWF:ROWH, :]
        half = ball[ROWH : ROWH + BLK, :]
        mid = slice(NHI + 128, NHI + 256)

        def ends(at, rows):
            prow[...] = prow[...] + dot(full, astack[at, :])
            prow[rows, :] = prow[rows, :] + dot(half, astack[mid, :])
            pcol[at, :] = turned(full, arow[...])
            pcol[mid, :] = turned(half, arow[rows, :])

        def rest(c):
            for q in range(4):
                beta = ball[ROWA + q * HI : ROWA + (q + 1) * HI, :]
                at = slice((4 * c + q) * 128, (4 * c + q + 1) * 128)
                pcol[at, :] = pcol[at, :] + turned(beta, arow[back, :])
                if c == 1:
                    prow[back, :] = prow[back, :] + dot(beta, astack[at, :])
                elif q == 3:
                    next_only = lax.broadcasted_iota(jnp.int32, (128, 256), 0) >= BLK - 384
                    a = jnp.where(next_only, astack[at, :].astype(F32), 0.0).astype(BF)
                    prow[back, :] = prow[back, :] + dot(beta, a)

        @pl.when(core == 0)
        def _():
            ends(slice(NHI, NHI + 128), own)
            rest(0)

        @pl.when(core == 1)
        def _():
            ends(slice(NHI + 256, LANES), slice(BLK, 2 * BLK))
            rest(1)

    ag_step(2, 1)
    ag_step(3, 1)
    ag_step(2, 2)
    ag_step(3, 2)
    p_first()
    ag_step(2, 3)
    ag_step(3, 3)
    p_second()

    pieces = (
        (0, prow, 0, BLK), (0, pcol, 0, BLK), (BLK, pcol, NLO, LO), (BLK + LO, pcol, NHI, HI),
        (2 * BLK, pcol, OLO, LO), (2 * BLK + LO, pcol, OHI, HI), (3 * BLK, prow, BLK, BLK),
    )
    mine = pl.ds(al(core * 128, 128), 128)
    other = pl.ds(al(128 - core * 128, 128), 128)
    for lanes, keep in ((other, False), (mine, True)):
        for to, src, at, n in pieces:
            v = src[at : at + n, lanes]
            if to == 0 and src is pcol:
                v = v + prow[own, lanes]
            elif to == 0:
                continue
            if keep:
                pown[to : to + n, :] = v
            else:
                psend[to : to + n, :] = v.astype(BF)
        if not keep:
            share = start("share", psend, precv, dev(fc=1))
    share.wait_recv()
    mcopies = []
    for i, where in ((1, dev(dx=2)), (0, dev(dx=1)), (2, dev(fy=1))):
        at = slice((i + 1) * BLK, (i + 2) * BLK)
        mout[i] = (pown[at, :] + precv[at, :].astype(F32)).astype(BF)
        mcopies.append((i, start(f"m{i}", mout.at[i], mrecv.at[i], where)))
    total = pown[own, :] + precv[own, :].astype(F32)
    for i, c in mcopies:
        c.wait_recv()
        total = total + mrecv[i].astype(F32)
    proj[...] = total.astype(BF).astype(F32)

    grad_copy.wait()
    zeros = [jnp.zeros((16, 128), F32) for _ in range(3)]
    energy = jnp.zeros((1, 128), F32)

    def body(step, carry):
        a0, a1, a2, e = carry
        rows = pl.ds(al(step * 16, 16), 16)
        pr = proj[rows, :]
        at = ats[core, rows, :].astype(F32)
        e = e + jnp.sum(pr * at, axis=0, keepdims=True)
        out = []
        for c, a in enumerate((a0, a1, a2)):
            for r in range(16):
                a = a + grads[c, step * 16 + r].astype(F32) * pr[r : r + 1, :]
            out.append(a)
        return (*out, e)

    a0, a1, a2, energy = lax.fori_loop(0, 25, body, (*zeros, energy))
    pr = proj[400:416, :]
    at = ats[core, 400:416, :].astype(F32)
    energy = energy + jnp.sum(pr * at, axis=0, keepdims=True)
    out = []
    for c, a in enumerate((a0, a1, a2)):
        for r in range(10):
            a = a + grads[c, 400 + r].astype(F32) * pr[r : r + 1, :]
        out.append(a)

    active = jnp.where(spec_ref[...] == 0, 1.0, 0.0)
    for c in range(3):
        pairs[c] = out[c] * active
    for n in range(16):
        mrow[0:3, n * 128 : (n + 1) * 128] = pairs[:, n, :]
    high = mrow[...].astype(BF)
    low = (mrow[...] - high.astype(F32)).astype(BF)
    spread = lax.dot_general(jnp.concatenate([high, low], axis=0), onehot[...], NT, preferred_element_type=F32)
    spread = -2.0 * (spread[0:8, :] + spread[8:16, :])
    fsend[0] = spread[:, 128:256]
    fsend[0, 0:3, :] = spread[0:3, 128:256] + 2.0 * jnp.sum(pairs[...], axis=1)
    fsend[0, 3:4, :] = energy * active
    fsend[1] = spread[:, 0:128]
    fsend[2] = spread[:, 256:384]

    for j in range(8):
        for kind, where in ((1, before), (2, after), (0, sp)):
            if j or kind:
                pltpu.make_async_remote_copy(
                    src_ref=fsend.at[kind], dst_ref=frecv.at[kind, col],
                    send_sem=fsem.at[min(kind, 1)], recv_sem=fsem.at[2 + min(kind, 1)],
                    device_id=(where, across[j]), device_id_type=MESH,
                ).start()
    frecv[0, col] = fsend[0]
    for c in sent:
        c.wait_send()
    fcopies = []
    for i, ref in ((0, frecv.at[0, 0:7]), (1, frecv.at[1:3])):
        fcopies.append(pltpu.make_async_remote_copy(
            src_ref=ref, dst_ref=ref, send_sem=fsem.at[i], recv_sem=fsem.at[2 + i], device_id=(sp, across[1]), device_id_type=MESH,
        ))
    for c in fcopies:
        c.wait_recv()
    summed = jnp.zeros((8, 128), F32)
    for kind in range(3):
        for j in range(8):
            summed = summed + frecv[kind, j]
    out_ref[...] = summed[0:4, :]

    assert len(names) <= NSEM
    for c in fcopies:
        c.wait_send()


def shards(env_desc, alpha, atom_desc, desc_grad, species, neighbors):
    vm = pl.BlockSpec(memory_space=pltpu.VMEM)
    V = pltpu.VMEM
    out = pl.pallas_call(
        kernel,
        out_shape=jax.ShapeDtypeStruct((4, 128), F32),
        in_specs=[pl.BlockSpec(memory_space=pl.ANY)] * 6,
        out_specs=vm,
        scratch_shapes=[
            V((1, 2048), F32), V((410, 128), BF), V((1, 128), jnp.int32), V((16, 128), jnp.int32),
            V((410, 2048), BF), V((OLO, 2048), BF), V((256, 2048), BF), V((LO, 1024), BF), V((256, 1024), BF),
            V((LO, 1024), BF), V((HI, 1024), BF), V((BLK, 2048), BF),
            V((2 * BLK, 2048), BF), V((2, ROWS, 128), F32), V((ROWS, 128), BF), V((ROWS, 128), BF),
            V((4, 576, 128), BF), V((4, 576, 128), BF), V((3, 576, 128), BF), V((3, 576, 128), BF),
            V((576, 128), F32), V((576, 128), BF), V((576, 128), BF), V((ROWS, 128), BF),
            V((2, 4 * BLK, 128), BF), V((LANES, 256), BF), V((2 * BLK, 256), BF),
            V((3, 410, 16, 128), BF), V((384, 2048), BF),
            V((2 * BLK, 256), F32), V((LANES, 256), F32), V((4 * BLK, 128), F32), V((4 * BLK, 128), BF), V((4 * BLK, 128), BF),
            V((3, BLK, 128), BF), V((3, BLK, 128), BF), V((BLK, 128), F32),
            V((3, 16, 128), F32), V((8, 2048), F32),
            V((3, 8, 128), F32), V((3, 8, 8, 128), F32),
            pltpu.SemaphoreType.DMA((6,)), pltpu.SemaphoreType.DMA((NSEM,)), pltpu.SemaphoreType.DMA((NSEM,)), pltpu.SemaphoreType.DMA((4,)),
        ],
        compiler_params=pltpu.CompilerParams(
            collective_id=0, has_side_effects=True, vmem_limit_bytes=58 * 2**20
        ),
    )(
        env_desc.T,
        alpha[None, :],
        atom_desc.T,
        species[None, :],
        neighbors.T,
        jnp.transpose(desc_grad, (2, 3, 1, 0)),
    )

    def outputs(both_ref, energy_ref, force_ref):
        energy_ref[...] = both_ref[3:4, :]
        force_ref[...] = both_ref[0:3, :]

    energies, forces = pl.pallas_call(
        outputs, out_shape=(jax.ShapeDtypeStruct((1, 128), F32), jax.ShapeDtypeStruct((3, 128), F32))
    )(out)
    return energies.reshape(128), forces


def solution(mesh):
    placed = (
        P("sp", "col"),
        P("sp"),
        P("sp", "col"),
        P("sp", None, None, "col"),
        P("sp"),
        P("sp", None),
    )
    return jax.shard_map(
        shards, mesh=mesh, in_specs=placed, out_specs=(P("sp"), P(None, "sp")), check_vma=False
    )
```

time: 110 us -> 104 us (0.945)
  Pallas kernels: 109 us -> 103 us
    pallas_call x1, Pallas kernels: 108 us -> 102 us  [shards(): pl.pallas_call(kernel, out_shape=jax.ShapeDtypeStruct((4, 128), F32), in_...]
where the time goes in v3:
time: 104 us; the launch traced here: 103 us
  Pallas kernels  103 us (99%)
    pallas_call x1, Pallas kernels, shards(): pl.pallas_call(kernel, out_shape=jax.ShapeDtypeStruct((4, 128), F32), in_...  102 us

profile of v3, /device:TPU:1, one launch (start us, length us, event | category | flops | bytes accessed | tf_op | source)
XLA Modules:
  0.0 103.5 jit_solution(81631977321048374)
XLA Ops:
  0.6 101.6 %shard_map.77.both_ref = f32[4,128]{1,0:T(4,128)} custom-call(bf16[410,2048]{1,0:T(8,128)(2,1)} %bitcast.8, f32[1,2048]{1,0:T(1,128)} %bitcast.10, bf16[410,128]{1,0:T(8,128)(2,1)} %bitcast.9, s32[1,128]{1,0:T(1,128)} %bitcast.12, s32[16,128]{1,0:T(8,128)} %bitcast.11, bf16[3,410,16,128]{3,2,1,0:T(8,128)(2,1)} %bitcast.7), custom_call_target="tpu_custom_call" | custom-call | tf_op jit(solution)/shard_map/pallas_call | solution.py:520
  102.2 1.3 %shard_map.78 = (f32[1,128]{1,0:T(1,128)}, f32[3,128]{1,0:T(4,128)}) custom-call(f32[4,128]{1,0:T(4,128)} %shard_map.77.both_ref), custom_call_target="tpu_custom_call" | custom-call | tf_op jit(solution)/shard_map/pallas_call | solution.py:556

commit v4 on v3

--- a/solution.py
+++ b/solution.py
@@ -11,13 +11,15 @@
 BF = jnp.bfloat16
 F32 = jnp.float32
 BLK = 416
-LO, HI = 256, 160
-KC, KD = 512, 1024
+LO, HI = 288, 128
+KC = 512
 ROW1 = BLK + LO
-ROWA, ROWF, ROWH, ROWS = 4 * ROW1, 4 * ROW1 + 4 * HI, 4 * ROW1 + 4 * HI + 2 * BLK, 4608
-CHS = (176, 160, 128, 112)
-OFF = (0, 8 * 176, ROWA, ROWA + 8 * 128)
-NLO, OLO, NHI, OHI, LANES = 416, 768, 1024, 1184, 1408
+ROWA, ROWS = 4 * ROW1, 4224
+ROWF = ROWA + 4 * HI
+ROWZ = ROWF + 2 * BLK
+CHS = (176, 176, 96, 80)
+OFF = (0, 1408, ROWA, ROWA + 8 * 96)
+NLO, OLO, OEND, NHI, OHI, LANES = 416, 704, 992, 1024, 1152, 1280
 NSEM = 128
 NT = (((1,), (1,)), ((), ()))
 TN = (((0,), (0,)), ((), ()))
@@ -26,7 +28,7 @@
 def kernel(
     env_ref, alpha_hbm, at_hbm, spec_hbm, nb_hbm, grad_ref,
     out_ref,
-    alpha_ref, at_ref, spec_ref, nb_ref, env, r1, nhi, olo, ohi, relay_lo, relay_hi, part, uw, acc, osend, orecv, rsp, rrp, rsm, rrm, csum, ysend, yrecv, ball,
+    alpha_ref, at_ref, spec_ref, nb_ref, env, r1, nhi, olo, ohi, relay_lo, relay_hi, part, uw, acc, osend, orecv, rsend, rrecv, csum, ysend, yrecv, ball,
     ats, astack, arow, grads, onehot, prow, pcol, pown, psend, precv, mout, mrecv, proj, pairs, mrow, fsend, frecv,
     lsem, ssem, rsem, fsem,
 ):
@@ -66,7 +68,7 @@
         small.append(pltpu.make_async_copy(src, dst, lsem.at[2 + i]))
         small[-1].start()
     peers = [dev(dx=1), dev(dx=-1), dev(dx=2), dev(fy=1), dev(dx=1, fy=1), dev(dx=-1, fy=1), dev(dx=2, fy=1)]
-    peers += [dev(fc=1), dev(fh=1), dev(dz=1), dev(dz=-1)]
+    peers += [dev(fc=1), dev(fh=1), dev(dz=1), dev(dz=-1), dev(dz=2), dev(dz=-2)]
     across = [(col + j) % 8 for j in range(8)]
     before, after = (sp + 31) % 32, (sp + 1) % 32
     peers += [(s, c) for s in (before, after) for c in across]
@@ -76,58 +78,57 @@
     env_copy.wait()
     grad_copy = pltpu.make_async_copy(grad_ref, grads, lsem.at[1])
     grad_copy.start()
-    r1[400:416, :] = jnp.zeros((16, 2048), BF)
-    r1[0:400, :] = env[0:400, :]
-    r1[400:410, :] = env[400:410, :]
+    for k in range(4):
+        lanes = slice(k * KC, (k + 1) * KC)
+        r1[k, 400:416, :] = jnp.zeros((16, KC), BF)
+        r1[k, 0:400, :] = env[0:400, lanes]
+        r1[k, 400:410, :] = env[400:410, lanes]
     pl.semaphore_wait(barrier, len(peers))
 
     def order(at_x):
-        t = jnp.where(at_x % 4 >= 2, 0, 1024)
-        return [al(o, KC) for o in (t, t + KC, 1024 - t, 1024 - t + KC)]
+        t = jnp.where(at_x % 4 >= 2, 0, 2)
+        return [t, t + 1, 2 - t, 3 - t]
 
     ks = order(x)
     ks_left = order(x + 3)
-    kh = [al(ks[0], KD), al(ks[2], KD)]
-    kh_left = [al(ks_left[0], KD), al(ks_left[2], KD)]
-    first = al(jnp.where(x < 2, 0, 1024), KD)
+    first = jnp.where(x < 2, 0, 2)
     own = slice(0, BLK)
     low_rows, high_rows = slice(0, LO), slice(LO, BLK)
     ys, yh_parts, os, rs = [], [], [], []
     for i in range(4):
-        ys.append(start(f"y{i}", r1.at[low_rows, pl.ds(ks[i], KC)], part.at[low_rows, pl.ds(ks[i], KC)], dev(fy=1)))
-        start(f"n{i}", r1.at[low_rows, pl.ds(ks_left[i], KC)], r1.at[NLO : NLO + LO, pl.ds(ks_left[i], KC)], dev(dx=-1))
+        ys.append(start(f"y{i}", r1.at[ks[i], low_rows, :], part.at[ks[i], low_rows, :], dev(fy=1)))
+        start(f"n{i}", r1.at[ks_left[i], low_rows, :], r1.at[ks_left[i], NLO : NLO + LO, :], dev(dx=-1))
         if i < 2:
-            os.append(start(f"o{i}", r1.at[low_rows, pl.ds(al(first + i * KC, KC), KC)], relay_lo.at[:, pl.ds(i * KC, KC)], dev(dx=1)))
-    for i in range(2):
-        yh_parts.append(start(f"yh{i}", r1.at[high_rows, pl.ds(kh[i], KD)], part.at[high_rows, pl.ds(kh[i], KD)], dev(fy=1)))
-        start(f"nh{i}", r1.at[high_rows, pl.ds(kh_left[i], KD)], nhi.at[0:HI, pl.ds(kh_left[i], KD)], dev(dx=-1))
+            os.append(start(f"o{i}", r1.at[first + i, low_rows, :], relay_lo.at[i], dev(dx=1)))
+    for i in range(4):
+        yh_parts.append(start(f"yh{i}", r1.at[ks[i], high_rows, :], part.at[ks[i], high_rows, :], dev(fy=1)))
+        start(f"nh{i}", r1.at[ks_left[i], high_rows, :], nhi.at[ks_left[i]], dev(dx=-1))
 
     def n_wait(i):
-        copy(f"n{i}", r1.at[low_rows, pl.ds(ks[i], KC)], r1.at[NLO : NLO + LO, pl.ds(ks[i], KC)], dev(dx=-1)).wait_recv()
+        copy(f"n{i}", r1.at[ks[i], low_rows, :], r1.at[ks[i], NLO : NLO + LO, :], dev(dx=-1)).wait_recv()
 
     def nh_wait(i):
-        copy(f"nh{i}", r1.at[high_rows, pl.ds(kh[i], KD)], nhi.at[0:HI, pl.ds(kh[i], KD)], dev(dx=-1)).wait_recv()
+        copy(f"nh{i}", r1.at[ks[i], high_rows, :], nhi.at[ks[i]], dev(dx=-1)).wait_recv()
 
     def pass_on(i):
         os[i].wait_recv()
         if i < 2:
-            rs.append(start(f"r{i}", relay_lo.at[:, pl.ds(i * KC, KC)], olo.at[:, pl.ds(i * KC, KC)], dev(dx=1)))
+            rs.append(start(f"r{i}", relay_lo.at[i], olo.at[i, 64 : 64 + LO, :], dev(dx=1)))
         else:
-            lanes = pl.ds((i - 2) * KC, KC)
-            rs.append(start(f"r{i}", relay_hi.at[:, lanes], ohi.at[32 : 32 + HI, lanes], dev(dx=1)))
+            rs.append(start(f"r{i}", relay_hi.at[i - 2], ohi.at[i - 2], dev(dx=1)))
 
     def o_high(i):
-        lanes = pl.ds((i - 2) * KC, KC)
-        src = r1.at[high_rows, pl.ds(al(first + (i - 2) * KC, KC), KC)]
-        os.append(start(f"o{i}", src, relay_hi.at[:, lanes], dev(dx=1)))
-
-    r1[NLO + LO : OLO, :] = jnp.zeros((OLO - NLO - LO, 2048), BF)
-    nhi[HI:256, :] = jnp.zeros((256 - HI, 2048), BF)
-    ohi[0:32, :] = jnp.zeros((32, 1024), BF)
-    ohi[32 + HI : 256, :] = jnp.zeros((224 - HI, 1024), BF)
+        os.append(start(f"o{i}", r1.at[first + i - 2, high_rows, :], relay_hi.at[i - 2], dev(dx=1)))
+
+    for k in range(4):
+        r1[k, OLO:768, :] = jnp.zeros((768 - OLO, KC), BF)
+    for k in range(2):
+        olo[k, 0:64, :] = jnp.zeros((64, KC), BF)
+        olo[k, 64 + LO : 384, :] = jnp.zeros((320 - LO, KC), BF)
     for c in small:
         c.wait()
-    uw[own, :] = (r1[own, :].astype(F32) * alpha_ref[...]).astype(BF)
+    for k in range(4):
+        uw[k, own, :] = (r1[k, own, :].astype(F32) * alpha_ref[:, k * KC : (k + 1) * KC]).astype(BF)
     slots = lax.broadcasted_iota(jnp.int32, (384, 128), 0)
     for n in range(16):
         onehot[:, n * 128 : (n + 1) * 128] = jnp.where(slots == nb_ref[n : n + 1, :], 1.0, 0.0).astype(BF)
@@ -135,7 +136,7 @@
     prow[...] = jnp.zeros_like(prow)
     pcol[...] = jnp.zeros_like(pcol)
     for c in (0, 1):
-        acc[c, ROWH + BLK : ROWS, :] = jnp.zeros((ROWS - ROWH - BLK, 128), F32)
+        acc[c, ROWZ:ROWS, :] = jnp.zeros((ROWS - ROWZ, 128), F32)
     ats[core, 400:416, :] = jnp.zeros((16, 128), BF)
     ats[core, 0:400, :] = at_ref[0:400, :]
     ats[core, 400:410, :] = at_ref[400:410, :]
@@ -147,17 +148,20 @@
         acc[c, at, :] = acc[c, at, :] + v if (c, row) in filled else v
         filled.add((c, row))
 
-    def weigh(rows, k, n):
+    def weigh(rows, k):
         at = slice(BLK + rows.start, BLK + rows.stop)
-        uw[at, pl.ds(k, n)] = (part[rows, pl.ds(k, n)].astype(F32) * alpha_ref[:, pl.ds(k, n)]).astype(BF)
-
-    def product(rows, rhs, r0, k, rk, n):
-        return lax.dot_general(
-            uw[rows, pl.ds(k, n)], rhs[r0 : r0 + 256, pl.ds(rk, n)], NT, preferred_element_type=F32
-        )
+        weight = alpha_ref[:, pl.ds(al(k * KC, KC), KC)]
+        uw[k, at, :] = (part[k, rows, :].astype(F32) * weight).astype(BF)
+
+    def product(rows, rhs, r0, n, steps):
+        v = None
+        for k, rk in steps:
+            d = lax.dot_general(uw[k, rows, :], rhs[rk, r0 : r0 + n, :], NT, preferred_element_type=F32)
+            v = d if v is None else v + d
+        return v
 
     def panels(v, t, base, stride):
-        for j in (0, 1):
+        for j in range(v.shape[1] // 128):
             add((t + j) // 4, base + (t + j) % 4 * stride, v[:, j * 128 : (j + 1) * 128])
 
     front, back, every = slice(0, ROW1), slice(ROW1, 2 * BLK), slice(0, 2 * BLK)
@@ -165,34 +169,31 @@
     def low_step(i):
         ys[i].wait_recv()
         n_wait(i)
-        weigh(low_rows, ks[i], KC)
+        weigh(low_rows, ks[i])
         for t in (0, 2, 4):
-            panels(product(front, r1, t * 128, ks[i], ks[i], KC), t, 0, ROW1)
+            panels(product(front, r1, t * 128, 256, ((ks[i], ks[i]),)), t, 0, ROW1)
 
     def low_opposite(j):
         rs[j].wait_recv()
-        panels(product(front, olo, 0, ks[j], j * KC, KC), 6, 0, ROW1)
+        panels(product(front, olo, 0, 384, ((ks[j], j),)), 5, 0, ROW1)
 
     def high_step(i):
-        yh_parts[i].wait_recv()
-        nh_wait(i)
-        weigh(high_rows, kh[i], KD)
+        two = ks[2 * i : 2 * i + 2]
+        for j, k in enumerate(two):
+            yh_parts[2 * i + j].wait_recv()
+            nh_wait(2 * i + j)
+            weigh(high_rows, k)
+        steps = [(k, k) for k in two]
         for t in (0, 2, 4):
-            panels(product(back, r1, t * 128, kh[i], kh[i], KD), t, ROWA, HI)
+            panels(product(back, r1, t * 128, 256, steps), t, ROWA, HI)
         if i == 0:
-            panels(product(back, olo, 0, kh[0], 0, KD), 6, ROWA, HI)
-        v = product(every, nhi, 0, kh[i], kh[i], KD)
-        add(0, ROWF, v[:, 0:128])
-        add(0, ROWH, v[0:BLK, 128:256])
-        add(1, ROWH, v[BLK : 2 * BLK, 128:256])
+            panels(product(back, olo, 0, 384, ((ks[0], 0), (ks[1], 1))), 5, ROWA, HI)
+        add(0, ROWF, product(every, nhi, 0, HI, steps))
 
     def high_opposite():
         rs[2].wait_recv()
         rs[3].wait_recv()
-        v = product(every, ohi, 0, kh[0], 0, KD)
-        add(0, ROWH, v[0:BLK, 0:128])
-        add(1, ROWH, v[BLK : 2 * BLK, 0:128])
-        add(1, ROWF, v[:, 128:256])
+        add(1, ROWF, product(every, ohi, 0, HI, ((ks[0], 0), (ks[1], 1))))
 
     cores = []
 
@@ -209,61 +210,121 @@
     def local(g, d):
         return acc[core, chunk(g, d), :] + orecv[chunk(g, d), :].astype(F32)
 
-    live = {}
-
-    def ring(g, far):
-        return (1 if far == 4 else -1) * (1 if g % 2 == 0 else -1)
-
-    def rs_send(g, s):
-        if s == 0 and g % 2 == 0:
+    def side(g):
+        return 1 if g % 2 == 0 else -1
+
+    routes = ((-4, -2), (-3, -1), (3, 1), (-1, -1), (1, 1), (-2, -2), (2, 2))
+
+    def rs_copy(g, i):
+        return copy(f"s{g}{i}", rsend.at[i, slot(g), :], rrecv.at[i, slot(g), :], dev(dz=side(g) * routes[i][1]))
+
+    def rs_first(g):
+        if g % 2 == 0:
             cores[g // 2].wait_recv()
-        for far, sbuf, rbuf in ((4, rsp, rrp), (3, rsm, rrm)):
-            if s >= far:
-                continue
-            way = ring(g, far)
-            v = local(g, z + way * (far - s))
-            if s:
-                live[g, far, s - 1].wait_recv()
-                v = v + rbuf[s - 1, slot(g), :].astype(F32)
-            sbuf[s, slot(g), :] = v.astype(BF)
-            live[g, far, s] = start(f"s{far}{g}{s}", sbuf.at[s, slot(g), :], rbuf.at[s, slot(g), :], dev(dz=way))
+        for i in range(5):
+            rsend[i, slot(g), :] = local(g, z + side(g) * routes[i][0]).astype(BF)
+            c = rs_copy(g, i)
+            c.start()
+            sent.append(c)
+
+    def rs_next(g):
+        for i, came in ((5, (0, 1)), (6, (2,))):
+            v = local(g, z + side(g) * routes[i][0])
+            for j in came:
+                rs_copy(g, j).wait_recv()
+                v = v + rrecv[j, slot(g), :].astype(F32)
+            rsend[i, slot(g), :] = v.astype(BF)
+            c = rs_copy(g, i)
+            c.start()
+            sent.append(c)
+
+    def first_rows(g, d):
+        return pl.ds(al(g * OFF[1] + ((d + 8) % 8) * CHS[0], 16), CHS[0])
+
+    def first_end():
+        for g in (0, 1):
+            for j in (3, 4, 5, 6):
+                rs_copy(g, j).wait_recv()
+        for g, keep in ((1 - yh, False), (yh, True)):
+            rows, at = first_rows(g, z), pl.ds(al(g * CHS[0], 16), CHS[0])
+            v = acc[core, rows, :] + orecv[rows, :].astype(F32)
+            for j in (3, 4, 5, 6):
+                v = v + rrecv[j, at, :].astype(F32)
+            if keep:
+                csum[0 : CHS[0], :] = v
+            else:
+                ysend[0 : CHS[0], :] = v.astype(BF)
+                ycopies[0] = start("h0", ysend.at[0 : CHS[0], :], yrecv.at[0 : CHS[0], :], dev(fh=1))
 
     ycopies = {}
 
     def rs_end(g):
-        live[g, 4, 3].wait_recv()
-        live[g, 3, 2].wait_recv()
-        v = local(g, z) + rrp[3, slot(g), :].astype(F32) + rrm[2, slot(g), :].astype(F32)
+        v = local(g, z)
+        for j in (3, 4, 5, 6):
+            rs_copy(g, j).wait_recv()
+            v = v + rrecv[j, slot(g), :].astype(F32)
         csum[slot(g), :] = v
         ysend[slot(g), :] = v.astype(BF)
         ycopies[g] = start(f"h{g}", ysend.at[slot(g), :], yrecv.at[slot(g), :], dev(fh=1))
 
-    def ag_start(g):
+    legs = ((0, 2), (0, -2), (0, 1), (0, -1), (-2, 2), (-2, 1), (2, -1))
+
+    turn = 1 - 2 * core
+
+    def ag_copy(g, i, recv=0):
+        at, to = legs[i]
+        if g == 0:
+            ref = ball.at[first_rows(yh, z + turn * (at - recv * to)), :]
+            return copy(f"g{g}{i}", ref, ref, dev(dz=turn * to))
+        ref = ball.at[chunk(g, z + side(g) * (at - recv * to)), :]
+        return copy(f"g{g}{i}", ref, ref, dev(dz=side(g) * to))
+
+    def ag_send(g, legs_of):
+        for i in legs_of:
+            c = ag_copy(g, i)
+            c.start()
+            sent.append(c)
+
+    def ag_first(g):
         ycopies[g].wait_recv()
-        ball[chunk(g, z), :] = (csum[slot(g), :] + yrecv[slot(g), :].astype(F32)).astype(BF)
-        ag_step(g, 0)
-
-    def ag_copy(g, s, far, recv=0):
-        ref = ball.at[chunk(g, z - ring(g, far) * (s + recv)), :]
-        return copy(f"g{far}{g}{s}", ref, ref, dev(dz=ring(g, far)))
-
-    def ag_step(g, s):
-        for far in (4, 3):
-            if s < far:
-                if s:
-                    ag_copy(g, s - 1, far, 1).wait_recv()
-                c = ag_copy(g, s, far)
-                c.start()
-                sent.append(c)
+        own_chunk = first_rows(yh, z) if g == 0 else chunk(g, z)
+        ball[own_chunk, :] = (csum[slot(g), :] + yrecv[slot(g), :].astype(F32)).astype(BF)
+        ag_send(g, (0, 1, 2, 3))
+        if g == 0:
+            over_send((7,))
+
+    def ag_next(g):
+        ag_copy(g, 0, 1).wait_recv()
+        ag_send(g, (4, 5))
+        ag_copy(g, 1, 1).wait_recv()
+        ag_send(g, (6,))
+
+    places = [at - to for at, to in legs] + [0]
+
+    def over(i, where):
+        ref = ball.at[first_rows(where, z + turn * places[i]), :]
+        return copy(f"v{i}", ref, ref, dev(fh=1))
+
+    def over_send(own_legs, waits=True):
+        for i in own_legs:
+            if i < 7 and waits:
+                ag_copy(0, i, 1).wait_recv()
+            c = over(i, yh)
+            c.start()
+            sent.append(c)
+
+    def over_wait():
+        for i in range(8):
+            over(i, 1 - yh).wait_recv()
 
     def ag_end(g):
-        for far in (4, 3):
-            ag_copy(g, far - 1, far, 1).wait_recv()
+        for i in (2, 3, 4, 5, 6):
+            ag_copy(g, i, 1).wait_recv()
 
     pass_on(0)
-    o_high(2)
     low_step(0)
     pass_on(1)
+    o_high(2)
     o_high(3)
     low_step(1)
     low_step(2)
@@ -272,48 +333,35 @@
     low_opposite(1)
     core_send(slice(0, ROWA))
     pass_on(2)
-    rs_send(0, 0)
-    rs_send(1, 0)
+    rs_first(0)
+    rs_first(1)
     pass_on(3)
-    rs_send(0, 1)
-    rs_send(1, 1)
     high_step(0)
-    rs_send(0, 2)
-    rs_send(1, 2)
+    rs_next(0)
+    rs_next(1)
     high_step(1)
     high_opposite()
     core_send(slice(ROWA, ROWS))
+    rs_first(2)
+    rs_first(3)
+    first_end()
     own_at = ats.at[core, own, :]
     acopies = [
         start("an", own_at, ats.at[core, BLK : 2 * BLK, :], dev(dx=-1)),
         start("ao", own_at, ats.at[core, 2 * BLK : 3 * BLK, :], dev(dx=2)),
         start("ap", own_at, ats.at[core, 3 * BLK : 4 * BLK, :], dev(fy=1)),
     ]
-    rs_send(0, 3)
-    rs_send(1, 3)
-    rs_send(2, 0)
-    rs_send(3, 0)
-    rs_end(0)
-    rs_end(1)
-    rs_send(2, 1)
-    rs_send(3, 1)
-    ag_start(0)
-    ag_start(1)
-    rs_send(2, 2)
-    rs_send(3, 2)
-    ag_step(0, 1)
-    ag_step(1, 1)
+    rs_next(2)
+    rs_next(3)
+    ag_first(0)
     for c in acopies:
         c.wait_recv()
     hand = start("hand", ats.at[core], ats.at[core], dev(fc=1))
-    rs_send(2, 3)
-    rs_send(3, 3)
-    ag_step(0, 2)
-    ag_step(1, 2)
     rs_end(2)
     rs_end(3)
-    ag_step(0, 3)
-    ag_step(1, 3)
+    ag_next(0)
+    over_send((0, 1), False)
+    over_send((2, 3))
     copy("hand", ats.at[1 - core], ats.at[1 - core], dev(fc=1)).wait_recv()
 
     def block(i, rows=own):
@@ -323,14 +371,14 @@
     arow[own, :] = both[block(0), :]
     arow[BLK : 2 * BLK, :] = both[block(3), :]
     astack[own, :] = both[block(0), :]
-    astack[NLO : NLO + LO, :] = both[block(1, low_rows), :]
-    astack[NLO + LO : OLO, :] = jnp.zeros((OLO - NLO - LO, 256), BF)
-    astack[OLO:NHI, :] = both[block(2, low_rows), :]
+    astack[NLO:OLO, :] = both[block(1, low_rows), :]
+    astack[OLO:OEND, :] = both[block(2, low_rows), :]
+    astack[OEND:NHI, :] = jnp.zeros((NHI - OEND, 256), BF)
     astack[NHI:OHI, :] = both[block(1, high_rows), :]
-    astack[OHI : OHI + HI, :] = both[block(2, high_rows), :]
-    astack[OHI + HI : LANES, :] = jnp.zeros((LANES - OHI - HI, 256), BF)
-    ag_start(2)
-    ag_start(3)
+    astack[OHI:LANES, :] = both[block(2, high_rows), :]
+    ag_first(2)
+    ag_first(3)
+    over_send((4, 6, 5))
 
     def dot(a, b):
         return jnp.dot(a, b, preferred_element_type=F32)
@@ -339,8 +387,7 @@
         return lax.dot_general(a, b, TN, preferred_element_type=F32)
 
     def p_first():
-        ag_end(0)
-        ag_end(1)
+        over_wait()
 
         @pl.when(core == 0)
         def _():
@@ -371,15 +418,11 @@
     def p_second():
         ag_end(2)
         ag_end(3)
-        full = ball[ROWF:ROWH, :]
-        half = ball[ROWH : ROWH + BLK, :]
-        mid = slice(NHI + 128, NHI + 256)
-
-        def ends(at, rows):
+        full = ball[ROWF:ROWZ, :]
+
+        def ends(at):
             prow[...] = prow[...] + dot(full, astack[at, :])
-            prow[rows, :] = prow[rows, :] + dot(half, astack[mid, :])
             pcol[at, :] = turned(full, arow[...])
-            pcol[mid, :] = turned(half, arow[rows, :])
 
         def rest(c):
             for q in range(4):
@@ -395,21 +438,17 @@
 
         @pl.when(core == 0)
         def _():
-            ends(slice(NHI, NHI + 128), own)
+            ends(slice(NHI, OHI))
             rest(0)
 
         @pl.when(core == 1)
         def _():
-            ends(slice(NHI + 256, LANES), slice(BLK, 2 * BLK))
+            ends(slice(OHI, LANES))
             rest(1)
 
-    ag_step(2, 1)
-    ag_step(3, 1)
-    ag_step(2, 2)
-    ag_step(3, 2)
+    ag_next(2)
+    ag_next(3)
     p_first()
-    ag_step(2, 3)
-    ag_step(3, 3)
     p_second()
 
     pieces = (
@@ -524,11 +563,11 @@
         out_specs=vm,
         scratch_shapes=[
             V((1, 2048), F32), V((410, 128), BF), V((1, 128), jnp.int32), V((16, 128), jnp.int32),
-            V((410, 2048), BF), V((OLO, 2048), BF), V((256, 2048), BF), V((LO, 1024), BF), V((256, 1024), BF),
-            V((LO, 1024), BF), V((HI, 1024), BF), V((BLK, 2048), BF),
-            V((2 * BLK, 2048), BF), V((2, ROWS, 128), F32), V((ROWS, 128), BF), V((ROWS, 128), BF),
-            V((4, 576, 128), BF), V((4, 576, 128), BF), V((3, 576, 128), BF), V((3, 576, 128), BF),
-            V((576, 128), F32), V((576, 128), BF), V((576, 128), BF), V((ROWS, 128), BF),
+            V((410, 2048), BF), V((4, 768, KC), BF), V((4, HI, KC), BF), V((2, 384, KC), BF), V((2, HI, KC), BF),
+            V((2, LO, KC), BF), V((2, HI, KC), BF), V((4, BLK, KC), BF),
+            V((4, 2 * BLK, KC), BF), V((2, ROWS, 128), F32), V((ROWS, 128), BF), V((ROWS, 128), BF),
+            V((7, 528, 128), BF), V((7, 528, 128), BF),
+            V((528, 128), F32), V((528, 128), BF), V((528, 128), BF), V((ROWS, 128), BF),
             V((2, 4 * BLK, 128), BF), V((LANES, 256), BF), V((2 * BLK, 256), BF),
             V((3, 410, 16, 128), BF), V((384, 2048), BF),
             V((2 * BLK, 256), F32), V((LANES, 256), F32), V((4 * BLK, 128), F32), V((4 * BLK, 128), BF), V((4 * BLK, 128), BF),

time: 104 us -> 94.4 us (0.908)
  Pallas kernels: 103 us -> 93.6 us
    pallas_call x1, Pallas kernels: 102 us -> 92.4 us  [shards(): pl.pallas_call(kernel, out_shape=jax.ShapeDtypeStruct((4, 128), F32), in_...]
where the time goes in v4:
time: 94.4 us; the launch traced here: 94.3 us
  Pallas kernels  93.6 us (99%)
    pallas_call x1, Pallas kernels, shards(): pl.pallas_call(kernel, out_shape=jax.ShapeDtypeStruct((4, 128), F32), in_...  92.4 us

profile of v4, /device:TPU:1, one launch (start us, length us, event | category | flops | bytes accessed | tf_op | source)
XLA Modules:
  0.0 94.3 jit_solution(9350022150160898321)
XLA Ops:
  0.6 92.4 %shard_map.77.both_ref = f32[4,128]{1,0:T(4,128)} custom-call(bf16[410,2048]{1,0:T(8,128)(2,1)} %bitcast.8, f32[1,2048]{1,0:T(1,128)} %bitcast.10, bf16[410,128]{1,0:T(8,128)(2,1)} %bitcast.9, s32[1,128]{1,0:T(1,128)} %bitcast.12, s32[16,128]{1,0:T(8,128)} %bitcast.11, bf16[3,410,16,128]{3,2,1,0:T(8,128)(2,1)} %bitcast.7), custom_call_target="tpu_custom_call" | custom-call | tf_op jit(solution)/shard_map/pallas_call | solution.py:559
  93.0 1.3 %shard_map.78 = (f32[1,128]{1,0:T(1,128)}, f32[3,128]{1,0:T(4,128)}) custom-call(f32[4,128]{1,0:T(4,128)} %shard_map.77.both_ref), custom_call_target="tpu_custom_call" | custom-call | tf_op jit(solution)/shard_map/pallas_call | solution.py:595

commit v5 on v4

--- a/solution.py
+++ b/solution.py
@@ -20,7 +20,7 @@
 CHS = (176, 176, 96, 80)
 OFF = (0, 1408, ROWA, ROWA + 8 * 96)
 NLO, OLO, OEND, NHI, OHI, LANES = 416, 704, 992, 1024, 1152, 1280
-NSEM = 128
+NSEND, NRECV = 24, 60
 NT = (((1,), (1,)), ((), ()))
 TN = (((0,), (0,)), ((), ()))
 
@@ -42,21 +42,26 @@
         k = 1 - core if fc else core
         return ((((z + dz + 8) % 8) * 2 + h) * 2 + k, a * 4 + (x + dx + 4) % 4)
 
-    names = {}
-    sent = []
-
-    def copy(name, src, dst, where):
-        i = names.setdefault(name, len(names))
+    sends, recvs = {}, {}
+
+    def copy(name, src, dst, where, out=None, into=None):
+        i = sends.setdefault(out or name, len(sends))
+        j = recvs.setdefault(into or name, len(recvs))
         return pltpu.make_async_remote_copy(
-            src_ref=src, dst_ref=dst, send_sem=ssem.at[i], recv_sem=rsem.at[i],
+            src_ref=src, dst_ref=dst, send_sem=ssem.at[i], recv_sem=rsem.at[j],
             device_id=where, device_id_type=MESH,
         )
 
-    def start(name, src, dst, where):
-        c = copy(name, src, dst, where)
+    def start(name, src, dst, where, out=None, into=None):
+        c = copy(name, src, dst, where, out, into)
         c.start()
-        sent.append(c)
         return c
+
+    def came(into, ref):
+        copy(None, ref, ref, dev(fc=1), next(iter(sends)), into).wait_recv()
+
+    def left(out, ref):
+        copy(None, ref, ref, dev(fc=1), out, next(iter(recvs))).wait_send()
 
     def al(v, m):
         return pl.multiple_of(v, m)
@@ -96,29 +101,29 @@
     low_rows, high_rows = slice(0, LO), slice(LO, BLK)
     ys, yh_parts, os, rs = [], [], [], []
     for i in range(4):
-        ys.append(start(f"y{i}", r1.at[ks[i], low_rows, :], part.at[ks[i], low_rows, :], dev(fy=1)))
-        start(f"n{i}", r1.at[ks_left[i], low_rows, :], r1.at[ks_left[i], NLO : NLO + LO, :], dev(dx=-1))
+        ys.append(start(f"y{i}", r1.at[ks[i], low_rows, :], part.at[ks[i], low_rows, :], dev(fy=1), "y"))
+        start(f"n{i}", r1.at[ks_left[i], low_rows, :], r1.at[ks_left[i], NLO : NLO + LO, :], dev(dx=-1), "n")
         if i < 2:
-            os.append(start(f"o{i}", r1.at[first + i, low_rows, :], relay_lo.at[i], dev(dx=1)))
+            os.append(start(f"o{i}", r1.at[first + i, low_rows, :], relay_lo.at[i], dev(dx=1), "o"))
     for i in range(4):
-        yh_parts.append(start(f"yh{i}", r1.at[ks[i], high_rows, :], part.at[ks[i], high_rows, :], dev(fy=1)))
-        start(f"nh{i}", r1.at[ks_left[i], high_rows, :], nhi.at[ks_left[i]], dev(dx=-1))
+        yh_parts.append(start(f"yh{i}", r1.at[ks[i], high_rows, :], part.at[ks[i], high_rows, :], dev(fy=1), "y"))
+        start(f"nh{i}", r1.at[ks_left[i], high_rows, :], nhi.at[ks_left[i]], dev(dx=-1), "n")
 
     def n_wait(i):
-        copy(f"n{i}", r1.at[ks[i], low_rows, :], r1.at[ks[i], NLO : NLO + LO, :], dev(dx=-1)).wait_recv()
+        copy(f"n{i}", r1.at[ks[i], low_rows, :], r1.at[ks[i], NLO : NLO + LO, :], dev(dx=-1), "n").wait_recv()
 
     def nh_wait(i):
-        copy(f"nh{i}", r1.at[ks[i], high_rows, :], nhi.at[ks[i]], dev(dx=-1)).wait_recv()
+        copy(f"nh{i}", r1.at[ks[i], high_rows, :], nhi.at[ks[i]], dev(dx=-1), "n").wait_recv()
 
     def pass_on(i):
         os[i].wait_recv()
         if i < 2:
-            rs.append(start(f"r{i}", relay_lo.at[i], olo.at[i, 64 : 64 + LO, :], dev(dx=1)))
+            rs.append(start(f"r{i}", relay_lo.at[i], olo.at[i, 64 : 64 + LO, :], dev(dx=1), "r"))
         else:
-            rs.append(start(f"r{i}", relay_hi.at[i - 2], ohi.at[i - 2], dev(dx=1)))
+            rs.append(start(f"r{i}", relay_hi.at[i - 2], ohi.at[i - 2], dev(dx=1), "r"))
 
     def o_high(i):
-        os.append(start(f"o{i}", r1.at[first + i - 2, high_rows, :], relay_hi.at[i - 2], dev(dx=1)))
+        os.append(start(f"o{i}", r1.at[first + i - 2, high_rows, :], relay_hi.at[i - 2], dev(dx=1), "o"))
 
     for k in range(4):
         r1[k, OLO:768, :] = jnp.zeros((768 - OLO, KC), BF)
@@ -178,28 +183,26 @@
         panels(product(front, olo, 0, 384, ((ks[j], j),)), 5, 0, ROW1)
 
     def high_step(i):
-        two = ks[2 * i : 2 * i + 2]
-        for j, k in enumerate(two):
-            yh_parts[2 * i + j].wait_recv()
-            nh_wait(2 * i + j)
-            weigh(high_rows, k)
-        steps = [(k, k) for k in two]
+        yh_parts[i].wait_recv()
+        nh_wait(i)
+        weigh(high_rows, ks[i])
+        steps = ((ks[i], ks[i]),)
         for t in (0, 2, 4):
             panels(product(back, r1, t * 128, 256, steps), t, ROWA, HI)
-        if i == 0:
-            panels(product(back, olo, 0, 384, ((ks[0], 0), (ks[1], 1))), 5, ROWA, HI)
+        if i < 2:
+            panels(product(back, olo, 0, 384, ((ks[i], i),)), 5, ROWA, HI)
         add(0, ROWF, product(every, nhi, 0, HI, steps))
 
-    def high_opposite():
-        rs[2].wait_recv()
-        rs[3].wait_recv()
-        add(1, ROWF, product(every, ohi, 0, HI, ((ks[0], 0), (ks[1], 1))))
-
-    cores = []
-
-    def core_send(rows):
+    def high_opposite(j):
+        rs[2 + j].wait_recv()
+        add(1, ROWF, product(every, ohi, 0, HI, ((ks[j], j),)))
+
+    cores = {}
+
+    def core_send(g, first, last):
+        rows = slice(first, last)
         osend[rows, :] = acc[1 - core, rows, :].astype(BF)
-        cores.append(start(f"core{rows.start}", osend.at[rows, :], orecv.at[rows, :], dev(fc=1)))
+        cores[g] = start(f"core{g}", osend.at[rows, :], orecv.at[rows, :], dev(fc=1))
 
     def chunk(g, d):
         return pl.ds(al(OFF[g] + ((d + 8) % 8) * CHS[g], 16), CHS[g])
@@ -216,35 +219,36 @@
     routes = ((-4, -2), (-3, -1), (3, 1), (-1, -1), (1, 1), (-2, -2), (2, 2))
 
     def rs_copy(g, i):
-        return copy(f"s{g}{i}", rsend.at[i, slot(g), :], rrecv.at[i, slot(g), :], dev(dz=side(g) * routes[i][1]))
+        into = f"s{g}a" if i < 2 else f"s{g}b" if i == 2 else f"s{g}c"
+        return copy(None, rsend.at[i, slot(g), :], rrecv.at[i, slot(g), :], dev(dz=side(g) * routes[i][1]), f"s{g}", into)
 
     def rs_first(g):
-        if g % 2 == 0:
-            cores[g // 2].wait_recv()
-        for i in range(5):
+        if g in cores:
+            cores[g].wait_recv()
+        for i in (1, 0, 2):
             rsend[i, slot(g), :] = local(g, z + side(g) * routes[i][0]).astype(BF)
-            c = rs_copy(g, i)
-            c.start()
-            sent.append(c)
+            rs_copy(g, i).start()
+
+    def rs_direct(g):
+        for i in (3, 4):
+            rsend[i, slot(g), :] = local(g, z + side(g) * routes[i][0]).astype(BF)
+            rs_copy(g, i).start()
 
     def rs_next(g):
-        for i, came in ((5, (0, 1)), (6, (2,))):
+        for i, arrived in ((5, (0, 1)), (6, (2,))):
             v = local(g, z + side(g) * routes[i][0])
-            for j in came:
-                rs_copy(g, j).wait_recv()
+            came(f"s{g}a" if i == 5 else f"s{g}b", rrecv.at[slice(0, 2) if i == 5 else slice(2, 3), slot(g), :])
+            for j in arrived:
                 v = v + rrecv[j, slot(g), :].astype(F32)
             rsend[i, slot(g), :] = v.astype(BF)
-            c = rs_copy(g, i)
-            c.start()
-            sent.append(c)
+            rs_copy(g, i).start()
 
     def first_rows(g, d):
         return pl.ds(al(g * OFF[1] + ((d + 8) % 8) * CHS[0], 16), CHS[0])
 
     def first_end():
         for g in (0, 1):
-            for j in (3, 4, 5, 6):
-                rs_copy(g, j).wait_recv()
+            came(f"s{g}c", rrecv.at[3:7, slot(g), :])
         for g, keep in ((1 - yh, False), (yh, True)):
             rows, at = first_rows(g, z), pl.ds(al(g * CHS[0], 16), CHS[0])
             v = acc[core, rows, :] + orecv[rows, :].astype(F32)
@@ -260,8 +264,8 @@
 
     def rs_end(g):
         v = local(g, z)
+        came(f"s{g}c", rrecv.at[3:7, slot(g), :])
         for j in (3, 4, 5, 6):
-            rs_copy(g, j).wait_recv()
             v = v + rrecv[j, slot(g), :].astype(F32)
         csum[slot(g), :] = v
         ysend[slot(g), :] = v.astype(BF)
@@ -273,17 +277,18 @@
 
     def ag_copy(g, i, recv=0):
         at, to = legs[i]
-        if g == 0:
-            ref = ball.at[first_rows(yh, z + turn * (at - recv * to)), :]
-            return copy(f"g{g}{i}", ref, ref, dev(dz=turn * to))
-        ref = ball.at[chunk(g, z + side(g) * (at - recv * to)), :]
-        return copy(f"g{g}{i}", ref, ref, dev(dz=side(g) * to))
+        into = f"g{g}{i}" if i < 2 else f"g{g}d" if g == 0 and i > 3 else f"g{g}c"
+        turned_to = turn if g == 0 else side(g)
+        place = z + turned_to * (at - recv * to)
+        ref = ball.at[first_rows(yh, place) if g == 0 else chunk(g, place), :]
+        return copy(None, ref, ref, dev(dz=turned_to * to), f"g{g}", into)
 
     def ag_send(g, legs_of):
         for i in legs_of:
-            c = ag_copy(g, i)
-            c.start()
-            sent.append(c)
+            ag_copy(g, i).start()
+
+    def ag_came(g, into, n):
+        came(f"g{g}{into}", ball.at[OFF[g] : OFF[g] + n * CHS[g], :])
 
     def ag_first(g):
         ycopies[g].wait_recv()
@@ -303,23 +308,19 @@
 
     def over(i, where):
         ref = ball.at[first_rows(where, z + turn * places[i]), :]
-        return copy(f"v{i}", ref, ref, dev(fh=1))
-
-    def over_send(own_legs, waits=True):
+        return copy("v", ref, ref, dev(fh=1))
+
+    def over_send(own_legs, into=None):
+        if into:
+            ag_came(0, into, len(own_legs))
         for i in own_legs:
-            if i < 7 and waits:
-                ag_copy(0, i, 1).wait_recv()
-            c = over(i, yh)
-            c.start()
-            sent.append(c)
+            over(i, yh).start()
 
     def over_wait():
-        for i in range(8):
-            over(i, 1 - yh).wait_recv()
+        came("v", ball.at[0 : OFF[1], :])
 
     def ag_end(g):
-        for i in (2, 3, 4, 5, 6):
-            ag_copy(g, i, 1).wait_recv()
+        ag_came(g, "c", 5)
 
     pass_on(0)
     low_step(0)
@@ -331,37 +332,44 @@
     low_opposite(0)
     low_step(3)
     low_opposite(1)
-    core_send(slice(0, ROWA))
+    core_send(0, 0, ROWA)
     pass_on(2)
     rs_first(0)
     rs_first(1)
+    rs_direct(0)
+    rs_direct(1)
     pass_on(3)
     high_step(0)
+    high_step(1)
     rs_next(0)
+    high_step(2)
+    high_opposite(0)
     rs_next(1)
-    high_step(1)
-    high_opposite()
-    core_send(slice(ROWA, ROWS))
+    high_step(3)
+    high_opposite(1)
+    core_send(2, ROWA, OFF[3])
+    core_send(3, OFF[3], ROWS)
+    own_at = ats.at[core, own, :]
+    for i, where in ((1, dev(dx=-1)), (2, dev(dx=2)), (3, dev(fy=1))):
+        start("a", own_at, ats.at[core, i * BLK : (i + 1) * BLK, :], where)
     rs_first(2)
     rs_first(3)
+    rs_direct(2)
+    rs_direct(3)
     first_end()
-    own_at = ats.at[core, own, :]
-    acopies = [
-        start("an", own_at, ats.at[core, BLK : 2 * BLK, :], dev(dx=-1)),
-        start("ao", own_at, ats.at[core, 2 * BLK : 3 * BLK, :], dev(dx=2)),
-        start("ap", own_at, ats.at[core, 3 * BLK : 4 * BLK, :], dev(fy=1)),
-    ]
     rs_next(2)
     rs_next(3)
     ag_first(0)
-    for c in acopies:
-        c.wait_recv()
-    hand = start("hand", ats.at[core], ats.at[core], dev(fc=1))
     rs_end(2)
     rs_end(3)
+    came("a", ats.at[core, BLK : 4 * BLK, :])
+    hand = start("hand", ats.at[core], ats.at[core], dev(fc=1))
     ag_next(0)
-    over_send((0, 1), False)
-    over_send((2, 3))
+    over_send((0, 1))
+    over_send((2, 3), "c")
+    ag_first(2)
+    ag_first(3)
+    over_send((4, 6, 5), "d")
     copy("hand", ats.at[1 - core], ats.at[1 - core], dev(fc=1)).wait_recv()
 
     def block(i, rows=own):
@@ -376,9 +384,6 @@
     astack[OEND:NHI, :] = jnp.zeros((NHI - OEND, 256), BF)
     astack[NHI:OHI, :] = both[block(1, high_rows), :]
     astack[OHI:LANES, :] = both[block(2, high_rows), :]
-    ag_first(2)
-    ag_first(3)
-    over_send((4, 6, 5))
 
     def dot(a, b):
         return jnp.dot(a, b, preferred_element_type=F32)
@@ -471,14 +476,13 @@
         if not keep:
             share = start("share", psend, precv, dev(fc=1))
     share.wait_recv()
-    mcopies = []
     for i, where in ((1, dev(dx=2)), (0, dev(dx=1)), (2, dev(fy=1))):
         at = slice((i + 1) * BLK, (i + 2) * BLK)
         mout[i] = (pown[at, :] + precv[at, :].astype(F32)).astype(BF)
-        mcopies.append((i, start(f"m{i}", mout.at[i], mrecv.at[i], where)))
+        start("m", mout.at[i], mrecv.at[i], where)
     total = pown[own, :] + precv[own, :].astype(F32)
-    for i, c in mcopies:
-        c.wait_recv()
+    came("m", mrecv)
+    for i in range(3):
         total = total + mrecv[i].astype(F32)
     proj[...] = total.astype(BF).astype(F32)
 
@@ -533,8 +537,21 @@
                     device_id=(where, across[j]), device_id_type=MESH,
                 ).start()
     frecv[0, col] = fsend[0]
-    for c in sent:
-        c.wait_send()
+    left("y", part)
+    left("n", part)
+    left("o", part.at[0:2])
+    left("r", part.at[0:2])
+    left("a", ats.at[core, BLK : 4 * BLK, :])
+    left("hand", ats.at[core])
+    left("share", psend)
+    left("m", mout)
+    left("v", ball.at[0 : OFF[1], :])
+    for g in (0, 2, 3):
+        cores[g].wait_send()
+        ycopies[g].wait_send()
+        left(f"g{g}", ball.at[OFF[g] : OFF[g] + 7 * CHS[g], :])
+    for g in range(4):
+        left(f"s{g}", rsend.at[:, slot(g), :])
     fcopies = []
     for i, ref in ((0, frecv.at[0, 0:7]), (1, frecv.at[1:3])):
         fcopies.append(pltpu.make_async_remote_copy(
@@ -548,7 +565,7 @@
             summed = summed + frecv[kind, j]
     out_ref[...] = summed[0:4, :]
 
-    assert len(names) <= NSEM
+    assert len(sends) <= NSEND and len(recvs) <= NRECV
     for c in fcopies:
         c.wait_send()
 
@@ -574,7 +591,7 @@
             V((3, BLK, 128), BF), V((3, BLK, 128), BF), V((BLK, 128), F32),
             V((3, 16, 128), F32), V((8, 2048), F32),
             V((3, 8, 128), F32), V((3, 8, 8, 128), F32),
-            pltpu.SemaphoreType.DMA((6,)), pltpu.SemaphoreType.DMA((NSEM,)), pltpu.SemaphoreType.DMA((NSEM,)), pltpu.SemaphoreType.DMA((4,)),
+            pltpu.SemaphoreType.DMA((6,)), pltpu.SemaphoreType.DMA((NSEND,)), pltpu.SemaphoreType.DMA((NRECV,)), pltpu.SemaphoreType.DMA((4,)),
         ],
         compiler_params=pltpu.CompilerParams(
             collective_id=0, has_side_effects=True, vmem_limit_bytes=58 * 2**20

time: 94.4 us -> 91 us (0.964)
  Pallas kernels: 93.6 us -> 90.2 us
    pallas_call x1, Pallas kernels: 92.4 us -> 89 us  [shards(): pl.pallas_call(kernel, out_shape=jax.ShapeDtypeStruct((4, 128), F32), in_...]
where the time goes in v5:
time: 91 us; the launch traced here: 90.9 us
  Pallas kernels  90.2 us (99%)
    pallas_call x1, Pallas kernels, shards(): pl.pallas_call(kernel, out_shape=jax.ShapeDtypeStruct((4, 128), F32), in_...  89 us

profile of v5, /device:TPU:1, one launch (start us, length us, event | category | flops | bytes accessed | tf_op | source)
XLA Modules:
  0.0 90.9 jit_solution(15940445968627430037)
XLA Ops:
  0.6 89.0 %shard_map.77.both_ref = f32[4,128]{1,0:T(4,128)} custom-call(bf16[410,2048]{1,0:T(8,128)(2,1)} %bitcast.8, f32[1,2048]{1,0:T(1,128)} %bitcast.10, bf16[410,128]{1,0:T(8,128)(2,1)} %bitcast.9, s32[1,128]{1,0:T(1,128)} %bitcast.12, s32[16,128]{1,0:T(8,128)} %bitcast.11, bf16[3,410,16,128]{3,2,1,0:T(8,128)(2,1)} %bitcast.7), custom_call_target="tpu_custom_call" | custom-call | tf_op jit(solution)/shard_map/pallas_call | solution.py:576
  89.6 1.3 %shard_map.78 = (f32[1,128]{1,0:T(1,128)}, f32[3,128]{1,0:T(4,128)}) custom-call(f32[4,128]{1,0:T(4,128)} %shard_map.77.both_ref), custom_call_target="tpu_custom_call" | custom-call | tf_op jit(solution)/shard_map/pallas_call | solution.py:612

commit v6 on v5

--- a/solution.py
+++ b/solution.py
@@ -27,7 +27,7 @@
 
 def kernel(
     env_ref, alpha_hbm, at_hbm, spec_hbm, nb_hbm, grad_ref,
-    out_ref,
+    energy_ref, force_ref,
     alpha_ref, at_ref, spec_ref, nb_ref, env, r1, nhi, olo, ohi, relay_lo, relay_hi, part, uw, acc, osend, orecv, rsend, rrecv, csum, ysend, yrecv, ball,
     ats, astack, arow, grads, onehot, prow, pcol, pown, psend, precv, mout, mrecv, proj, pairs, mrow, fsend, frecv,
     lsem, ssem, rsem, fsem,
@@ -294,7 +294,7 @@
         ycopies[g].wait_recv()
         own_chunk = first_rows(yh, z) if g == 0 else chunk(g, z)
         ball[own_chunk, :] = (csum[slot(g), :] + yrecv[slot(g), :].astype(F32)).astype(BF)
-        ag_send(g, (0, 1, 2, 3))
+        ag_send(g, (0, 1) if g else (0, 1, 2, 3))
         if g == 0:
             over_send((7,))
 
@@ -369,6 +369,8 @@
     over_send((2, 3), "c")
     ag_first(2)
     ag_first(3)
+    ag_send(2, (2, 3))
+    ag_send(3, (2, 3))
     over_send((4, 6, 5), "d")
     copy("hand", ats.at[1 - core], ats.at[1 - core], dev(fc=1)).wait_recv()
 
@@ -528,8 +530,8 @@
     fsend[1] = spread[:, 0:128]
     fsend[2] = spread[:, 256:384]
 
-    for j in range(8):
-        for kind, where in ((1, before), (2, after), (0, sp)):
+    for kind, where in ((1, before), (2, after), (0, sp)):
+        for j in (2, 6, 4, 3, 5, 1, 7, 0):
             if j or kind:
                 pltpu.make_async_remote_copy(
                     src_ref=fsend.at[kind], dst_ref=frecv.at[kind, col],
@@ -563,7 +565,8 @@
     for kind in range(3):
         for j in range(8):
             summed = summed + frecv[kind, j]
-    out_ref[...] = summed[0:4, :]
+    energy_ref[...] = summed[3:4, :]
+    force_ref[...] = summed[0:3, :]
 
     assert len(sends) <= NSEND and len(recvs) <= NRECV
     for c in fcopies:
@@ -573,11 +576,11 @@
 def shards(env_desc, alpha, atom_desc, desc_grad, species, neighbors):
     vm = pl.BlockSpec(memory_space=pltpu.VMEM)
     V = pltpu.VMEM
-    out = pl.pallas_call(
+    held = pl.pallas_call(
         kernel,
-        out_shape=jax.ShapeDtypeStruct((4, 128), F32),
+        out_shape=(jax.ShapeDtypeStruct((1, 128), F32), jax.ShapeDtypeStruct((3, 128), F32)),
         in_specs=[pl.BlockSpec(memory_space=pl.ANY)] * 6,
-        out_specs=vm,
+        out_specs=(vm, vm),
         scratch_shapes=[
             V((1, 2048), F32), V((410, 128), BF), V((1, 128), jnp.int32), V((16, 128), jnp.int32),
             V((410, 2048), BF), V((4, 768, KC), BF), V((4, HI, KC), BF), V((2, 384, KC), BF), V((2, HI, KC), BF),
@@ -605,13 +608,24 @@
         jnp.transpose(desc_grad, (2, 3, 1, 0)),
     )
 
-    def outputs(both_ref, energy_ref, force_ref):
-        energy_ref[...] = both_ref[3:4, :]
-        force_ref[...] = both_ref[0:3, :]
-
+    def outputs(energy_ref, force_ref, energy_out, force_out, sem):
+        copies = [
+            pltpu.make_async_copy(energy_ref, energy_out, sem.at[0]),
+            pltpu.make_async_copy(force_ref, force_out, sem.at[1]),
+        ]
+        for c in copies:
+            c.start()
+        for c in copies:
+            c.wait()
+
+    anywhere = pl.BlockSpec(memory_space=pl.ANY)
     energies, forces = pl.pallas_call(
-        outputs, out_shape=(jax.ShapeDtypeStruct((1, 128), F32), jax.ShapeDtypeStruct((3, 128), F32))
-    )(out)
+        outputs,
+        out_shape=(jax.ShapeDtypeStruct((1, 128), F32), jax.ShapeDtypeStruct((3, 128), F32)),
+        in_specs=[anywhere, anywhere],
+        out_specs=(anywhere, anywhere),
+        scratch_shapes=[pltpu.SemaphoreType.DMA((2,))],
+    )(*held)
     return energies.reshape(128), forces
 
 

time: 91 us -> 90.8 us (level)
  no operation moved by 1% of the time
where the time goes in v6:
time: 90.8 us; the launch traced here: 90.7 us
  Pallas kernels  90 us (99%)
    pallas_call x1, Pallas kernels, shards(): pl.pallas_call(kernel, out_shape=(jax.ShapeDtypeStruct((1, 128), F32), ja...  88.9 us

profile of v6, /device:TPU:1, one launch (start us, length us, event | category | flops | bytes accessed | tf_op | source)
XLA Modules:
  0.0 90.7 jit_solution(14899770841111059232)
XLA Ops:
  0.6 88.9 %shard_map.77 = (f32[1,128]{1,0:T(1,128)}, f32[3,128]{1,0:T(4,128)}) custom-call(bf16[410,2048]{1,0:T(8,128)(2,1)} %bitcast.8, f32[1,2048]{1,0:T(1,128)} %bitcast.10, bf16[410,128]{1,0:T(8,128)(2,1)} %bitcast.9, s32[1,128]{1,0:T(1,128)} %bitcast.12, s32[16,128]{1,0:T(8,128)} %bitcast.11, bf16[3,410,16,128]{3,2,1,0:T(8,128)(2,1)} %bitcast.7), custom_call_target="tpu_custom_call" | custom-call | tf_op jit(solution)/shard_map/pallas_call | solution.py:579
  89.5 1.2 %shard_map.78 = (f32[1,128]{1,0:T(1,128)}, f32[3,128]{1,0:T(4,128)}) custom-call(f32[1,128]{1,0:T(1,128)} %get-tuple-element.6.energy_ref, f32[3,128]{1,0:T(4,128)} %get-tuple-element.7.force_ref), custom_call_target="tpu_custom_call" | custom-call | tf_op jit(solution)/shard_map/pallas_call | solution.py:622
